TPU v7x, 128 devices: a whole 4x4x4 slice. The times are simulated.
128 devices in a mesh: idx: 64 (over y, x, z), enc: 2 (over core).
Axes of the slice: x: 4, y: 4, z: 4, core: 2. Of those that a mesh axis runs over, the one named last changes fastest.
Arguments:
- queries: bfloat16 [262144, 1024], P(('idx', 'enc')), may hold values from -12 to 12
- positives: bfloat16 [262144, 1024], P(('idx', 'enc')), may hold values from -6 to 6
- passages: bfloat16 [131072, 1024], P('idx'), may hold values from -12 to 12
- negatives: int32 [128, 2048], P(('idx', 'enc')), may hold values from -1 to 131071, as said below
Outputs:
- query_loss: float32 [262144], P(('idx', 'enc'))
- grad_queries: bfloat16 [262144, 1024], P(('idx', 'enc'))
- grad_passages: bfloat16 [131072, 1024], P('idx')
Inputs may be any that keep to these rules, and one draw needn't show every extreme that they name: `negatives`: -1 marks a padding slot. Of the 2048 slots of one device (its 1 row), at most 32 name passages of one index shard (ids 2048 * k to 2048 * k + 2047), and in every draw some shard is named exactly 32 times by every device.
All inputs are finite; a program needn't handle non-finite values.
Results may differ from a plain program's by a relative error of at most 0.0055.
Values may be sent and summed in bfloat16 or wider, within the bound.
A program may use at most 128 MiB of HBM per device.

v0:
```python
import math

import jax
import jax.numpy as jnp
from jax import lax
from jax.sharding import PartitionSpec as P

LSCALE = 32


masked_value = -1e30


def group_terms(query_block, positive_block, neg_rows, is_live, loss_scale):
    feature_dim = query_block.shape[1]
    logit_scale = 3.0 / math.sqrt(feature_dim)
    pos_logit = logit_scale * jnp.sum(
        query_block.astype(jnp.float32) * positive_block.astype(jnp.float32), axis=1
    )
    neg_logit = logit_scale * lax.dot_general(
        query_block, neg_rows, (((1,), (1,)), ((), ())), preferred_element_type=jnp.float32
    )
    masked = jnp.where(is_live[None, :], neg_logit, masked_value)
    top_logit = jnp.maximum(jnp.max(masked, axis=1), pos_logit)
    neg_exp = jnp.where(is_live[None, :], jnp.exp(masked - top_logit[:, None]), 0.0)
    pos_exp = jnp.exp(pos_logit - top_logit)
    norm_total = pos_exp + jnp.sum(neg_exp, axis=1)
    query_loss = top_logit + jnp.log(norm_total) - pos_logit
    factor = loss_scale * logit_scale
    weights = (factor * neg_exp / norm_total[:, None]).astype(jnp.bfloat16)
    grad_query = jnp.dot(weights, neg_rows, preferred_element_type=jnp.float32)
    grad_query = grad_query + (factor * (pos_exp / norm_total - 1.0))[
        :, None
    ] * positive_block.astype(jnp.float32)
    row_grad = lax.dot_general(
        weights, query_block, (((0,), (0,)), ((), ())), preferred_element_type=jnp.float32
    ).astype(jnp.bfloat16)
    return (query_loss, grad_query.astype(jnp.bfloat16), row_grad)


def scatter_rows(wanted, returned, shard_rows):
    feature_dim = returned.shape[-1]
    target = jnp.where(wanted >= 0, wanted, shard_rows).reshape(-1)
    addend = returned.reshape(-1, feature_dim).astype(jnp.float32)
    return jnp.zeros((shard_rows, feature_dim), jnp.float32).at[target].add(addend, mode="drop")


def local(queries, positives, passages, negatives):
    idx_count = lax.axis_size("idx")
    shard_rows = passages.shape[0]
    feature_dim = queries.shape[1]
    flat_ids = negatives.reshape(-1)
    list_len = flat_ids.shape[0]
    capacity = list_len // idx_count
    is_live = flat_ids >= 0
    owner_idx = jnp.where(is_live, flat_ids // shard_rows, idx_count)
    local_row = jnp.where(is_live, flat_ids % shard_rows, 0)
    one_hot = (owner_idx[:, None] == jnp.arange(idx_count, dtype=jnp.int32)[None, :]).astype(
        jnp.int32
    )
    slot_rank = jnp.sum((jnp.cumsum(one_hot, axis=0) - one_hot) * one_hot, axis=1)
    slot_pos = jnp.where(is_live, owner_idx * capacity + slot_rank, list_len)
    request = jnp.full((list_len + 1,), -1, jnp.int32).at[slot_pos].set(local_row)
    request = request[:list_len].reshape(idx_count, capacity)
    wanted = lax.all_to_all(request, "idx", split_axis=0, concat_axis=0, tiled=True)
    wanted_live = wanted >= 0
    picked = jnp.take(passages, jnp.maximum(wanted, 0).reshape(-1), axis=0)
    picked = jnp.where(wanted_live.reshape(-1, 1), picked, jnp.zeros_like(picked))
    picked = picked.reshape(idx_count, capacity, feature_dim)
    fetched = lax.all_to_all(picked, "idx", split_axis=0, concat_axis=0, tiled=True).reshape(
        list_len, feature_dim
    )
    gather_pos = jnp.minimum(slot_pos, list_len - 1)
    neg_rows = jnp.take(fetched, gather_pos, axis=0)
    query_loss, grad_query, row_grad = group_terms(queries, positives, neg_rows, is_live, LSCALE)
    send_back = jnp.zeros((list_len + 1, feature_dim), jnp.bfloat16).at[slot_pos].set(row_grad)
    send_back = send_back[:list_len].reshape(idx_count, capacity, feature_dim)
    returned = lax.all_to_all(send_back, "idx", split_axis=0, concat_axis=0, tiled=True)
    grad_shard = lax.psum(scatter_rows(wanted, returned, shard_rows), "enc")
    return (query_loss, grad_query, grad_shard.astype(jnp.bfloat16))


def solution(mesh):
    placed = (
        P(("idx", "enc"), None),
        P(("idx", "enc"), None),
        P("idx", None),
        P(("idx", "enc"), None),
    )
    return jax.shard_map(
        local,
        mesh=mesh,
        in_specs=placed,
        out_specs=(P(("idx", "enc")), P(("idx", "enc"), None), P("idx", None)),
        check_vma=False,
    )
```

profile of v0, /device:TPU:1, one launch (start us, length us, event | category | flops | bytes accessed | tf_op | source)
XLA Modules:
  0.0 304.2 jit_solution(13959994345473311394)
XLA Ops:
  0.6 0.8 fusion.18
  1.4 0.7 fusion.16
  2.2 18.1 %reduce-window.6 = s32[64,16,128]{2,1,0:T(8,128)S(1)} reduce-window(s32[64,16,128]{2,1,0:T(8,128)S(1)} %fusion.15, s32[]{:T(128)} %constant.26.clone.1), window={size=1x1x128 pad=0_0x0_0x127_0}, to_apply=%region_0.1 | reduce-window | flops 16646144 | bytes 1048580 | tf_op jit(solution)/shard_map/reduce-window
  21.7 8.1 %scatter_custom_fusion = s32[2049]{0:T(1024)S(1)} fusion(s32[2048]{0:T(1024)S(1)} %bitcast.58, s32[2048]{0:T(1024)S(1)} %get-tuple-element.10, s32[]{:T(128)} %constant.27.clone.1), kind=kCustom, calls=%fused_computation.73 | custom fusion | bytes 8200 | tf_op jit(solution)/shard_map/scatter | solution.py:63
  29.9 20.2 %all_to_all.22 = s32[64,1,32]{2,1,0:T(1,128)S(1)} all-to-all(s32[64,1,32]{2,1,0:T(1,128)S(1)} %bitcast.57), channel_id=1, replica_groups=mesh['idx'=64,'enc'=2] {'idx'}, dimensions={0} | all-to-all | bytes 16384 | tf_op jit(solution)/shard_map/all_to_all | solution.py:65
  50.5 0.8 fusion.31
  51.6 13.7 %gather_fusion = bf16[2048,1024]{1,0:T(8,128)(2,1)} fusion(bf16[2048,1024]{1,0:T(8,128)(2,1)} %param.8, s32[2048]{0:T(1024)S(1)} %fusion.24), kind=kCustom, calls=%fused_computation.clone | custom fusion | bytes 8396800 | tf_op jit(solution)/shard_map/jit(_take)/gather | solution.py:67
  65.3 4.0 %select_select_fusion = bf16[2048,1024]{1,0:T(8,128)(2,1)} fusion(bf16[2048,1024]{1,0:T(8,128)(2,1)} %gather_fusion, pred[2048]{0:T(1024)(128)(4,1)S(1)} %compare_and_fusion.1, pred[2048]{0:T(1024)(128)(4,1)S(1)} %ge.51), kind=kLoop, calls=%fused_computation.17 | loop fusion | flops 4194304 | bytes 8392704 | tf_op jit(solution)/shard_map/jit(_where)/select_n | solution.py:68
  69.3 5.8 %all-to-all-start.1 = ((bf16[64,32,1024]{2,1,0:T(8,128)(2,1)}), bf16[64,32,1024]{2,1,0:T(8,128)(2,1)}, u32[]{:S(2)}, u32[]{:S(2)}) async-start(bf16[64,32,1024]{2,1,0:T(8,128)(2,1)} %bitcast.48), calls=%async_computation.1 | async-start | bytes 8388608 | tf_op jit(solution)/shard_map/all_to_all | solution.py:70
  75.2 4.6 %fusion.2 = f32[2048]{0:T(1024)S(1)} fusion(bf16[2048,1024]{1,0:T(8,128)(2,1)} %param.7, bf16[2048,1024]{1,0:T(8,128)(2,1)} %param.6), kind=kLoop, calls=%fused_computation.12 | loop fusion | flops 8386560 | bytes 8396800 | tf_op jit(solution)/shard_map/reduce_sum | solution.py:17
  79.8 44.7 %all-to-all-done.1 = bf16[64,32,1024]{2,1,0:T(8,128)(2,1)} async-done(((bf16[64,32,1024]{2,1,0:T(8,128)(2,1)}), bf16[64,32,1024]{2,1,0:T(8,128)(2,1)}, u32[]{:S(2)}, u32[]{:S(2)}) %all-to-all-start.1) | async-done | bytes 4194336 | tf_op jit(solution)/shard_map/all_to_all | solution.py:70
  124.5 13.7 %gather_fusion.1 = bf16[2048,1024]{1,0:T(8,128)(2,1)} fusion(bf16[2048,1024]{1,0:T(8,128)(2,1)} %bitcast.10, s32[2048]{0:T(1024)S(1)} %get-tuple-element.9), kind=kCustom, calls=%fused_computation.1.clone | custom fusion | bytes 8396800 | tf_op jit(solution)/shard_map/jit(_take)/gather | solution.py:74
  138.2 12.0 %fusion = (f32[2048]{0:T(1024)S(1)}, f32[2048,2048]{1,0:T(8,128)S(1)}) fusion(pred[2048]{0:T(1024)(128)(4,1)S(1)} %compare_reduce_fusion.1, bf16[2048,1024]{1,0:T(8,128)(2,1)} %param.6, bf16[2048,1024]{1,0:T(8,128)(2,1)} %gather_fusion.1, pred[2048]{0:T(1024)(128)(4,1)S(1)} %compare_and_fusion), kind=kOutput, calls=%fused_computation.8 | convolution fusion | flops 8604612608 | bytes 25178112 | tf_op jit(solution)/shard_map/dot_general | solution.py:20
  150.2 5.8 %fusion.1 = f32[2048]{0:T(1024)S(1)} fusion(f32[2048,2048]{1,0:T(8,128)S(1)} %get-tuple-element.12, f32[2048]{0:T(1024)S(1)} %multiply_maximum_fusion, pred[2048]{0:T(1024)(128)(4,1)S(1)} %compare_reduce_fusion.1), kind=kLoop, calls=%fused_computation.9 | loop fusion | flops 20969472 | bytes 16795648 | tf_op jit(solution)/shard_map/reduce_sum | solution.py:27
  156.7 6.9 %divide_convert_fusion = bf16[2048,2048]{1,0:T(8,128)(2,1)S(1)} fusion(f32[2048,2048]{1,0:T(8,128)S(1)} %get-tuple-element.12, f32[2048]{0:T(1024)S(1)} %get-tuple-element.6, f32[2048]{0:T(1024)S(1)} %multiply_maximum_fusion, pred[2048]{0:T(1024)(128)(4,1)S(1)} %compare_reduce_fusion.1), kind=kLoop, calls=%fused_computation.5 | loop fusion | flops 29360128 | bytes 25184256 | tf_op jit(solution)/shard_map/convert_element_type | solution.py:30
  163.6 3.2 %copy-done = bf16[2048,2048]{1,0:T(8,128)(2,1)} copy-done((bf16[2048,2048]{1,0:T(8,128)(2,1)}, bf16[2048,2048]{1,0:T(8,128)(2,1)S(1)}, u32[]{:S(2)}) %copy-start) | copy-done | bytes 8388632
  166.8 11.0 %fusion.32 = f32[2048,1024]{1,0:T(8,128)} fusion(bf16[2048,2048]{1,0:T(8,128)(2,1)S(1)} %divide_convert_fusion, bf16[2048,1024]{1,0:T(8,128)(2,1)S(1)} %copy-done.1), kind=kOutput, calls=%fused_computation.82 | convolution fusion | flops 8589934592 | bytes 20971520 | tf_op jit(solution)/shard_map/dot_general | solution.py:35
  177.7 13.4 %scatter_custom_fusion.1 = bf16[2049,1024]{1,0:T(8,128)(2,1)} fusion(s32[2048]{0:T(1024)S(1)} %bitcast.59, f32[2048,1024]{1,0:T(8,128)} %fusion.32, bf16[]{:T(256)} %constant.66.clone.1), kind=kCustom, calls=%fused_computation.18 | custom fusion | flops 2097152 | bytes 12584962 | tf_op jit(solution)/shard_map/scatter | solution.py:76
  191.1 4.6 %slice.23 = bf16[2048,1024]{1,0:T(8,128)(2,1)} slice(bf16[2049,1024]{1,0:T(8,128)(2,1)} %scatter_custom_fusion.1), slice={[0:2048], [0:1024]} | slice | bytes 8388608 | tf_op jit(solution)/shard_map/slice | solution.py:77
  195.7 9.2 %all-to-all-start.2 = ((bf16[64,32,1024]{2,1,0:T(8,128)(2,1)}), bf16[64,32,1024]{2,1,0:T(8,128)(2,1)}, u32[]{:S(2)}, u32[]{:S(2)}) async-start(bf16[64,32,1024]{2,1,0:T(8,128)(2,1)} %bitcast.47), calls=%async_computation.2 | async-start | bytes 8388608 | tf_op jit(solution)/shard_map/all_to_all | solution.py:78
  205.1 15.6 %fusion.4 = bf16[2048,1024]{1,0:T(8,128)(2,1)} fusion(bf16[2048,1024]{1,0:T(8,128)(2,1)} %param.7, f32[2048]{0:T(1024)S(1)} %get-tuple-element.8, bf16[2048,2048]{1,0:T(8,128)(2,1)} %copy-done, bf16[2048,1024]{1,0:T(8,128)(2,1)} %gather_fusion.1, pred[2048]{0:T(1024)(128)(4,1)S(1)} %compare_and_fusion), kind=kOutput, calls=%fused_computation.14 | convolution fusion | flops 8600420352 | bytes 20981760 | tf_op jit(solution)/shard_map/dot_general | solution.py:31
  220.7 31.4 %all-to-all-done.2 = bf16[64,32,1024]{2,1,0:T(8,128)(2,1)} async-done(((bf16[64,32,1024]{2,1,0:T(8,128)(2,1)}), bf16[64,32,1024]{2,1,0:T(8,128)(2,1)}, u32[]{:S(2)}, u32[]{:S(2)}) %all-to-all-start.2) | async-done | bytes 4194336 | tf_op jit(solution)/shard_map/all_to_all | solution.py:78
  252.0 21.8 %scatter_custom_fusion.2 = f32[2048,1024]{1,0:T(8,128)} fusion(s32[2048]{0:T(1024)S(1)} %bitcast.60, bf16[2048,1024]{1,0:T(8,128)(2,1)} %bitcast.14, f32[]{:T(128)} %constant.70.clone.1), kind=kCustom, calls=%fused_computation.15 | custom fusion | flops 4194304 | bytes 12582916 | tf_op jit(solution)/shard_map/scatter-add | solution.py:45
  273.8 30.4 %all-reduce.1 = bf16[2048,1024]{1,0:T(8,128)(2,1)} all-reduce(f32[2048,1024]{1,0:T(8,128)} %scatter_custom_fusion.2), channel_id=1, replica_groups=mesh['idx'=64,'enc'=2] {'enc'}, use_global_device_ids=true, to_apply=%region_9.11 | all-reduce | flops 2097152 | bytes 12582912 | tf_op jit(solution)/shard_map/psum | solution.py:79
  (27 shorter events, 3.1 us)
Async XLA Ops:
  0.6 21.0 %copy-start.2 = (s32[1,2048]{1,0:T(1,128)S(1)}, s32[1,2048]{1,0:T(1,128)}, u32[]{:S(2)}) copy-start(s32[1,2048]{1,0:T(1,128)} %param.9) | copy-start | bytes 24580
  69.3 55.3 %all-to-all-start.1 = ((bf16[64,32,1024]{2,1,0:T(8,128)(2,1)}), bf16[64,32,1024]{2,1,0:T(8,128)(2,1)}, u32[]{:S(2)}, u32[]{:S(2)}) async-start(bf16[64,32,1024]{2,1,0:T(8,128)(2,1)} %bitcast.48), calls=%async_computation.1 | async-start | bytes 8388608 | tf_op jit(solution)/shard_map/all_to_all | solution.py:70
  156.7 10.1 %copy-start.1 = (bf16[2048,1024]{1,0:T(8,128)(2,1)S(1)}, bf16[2048,1024]{1,0:T(8,128)(2,1)}, u32[]{:S(2)}) copy-start(bf16[2048,1024]{1,0:T(8,128)(2,1)} %param.6) | copy-start | bytes 12582916
  163.6 3.2 %copy-start = (bf16[2048,2048]{1,0:T(8,128)(2,1)}, bf16[2048,2048]{1,0:T(8,128)(2,1)S(1)}, u32[]{:S(2)}) copy-start(bf16[2048,2048]{1,0:T(8,128)(2,1)S(1)} %divide_convert_fusion) | copy-start | bytes 25165828
  195.7 56.3 %all-to-all-start.2 = ((bf16[64,32,1024]{2,1,0:T(8,128)(2,1)}), bf16[64,32,1024]{2,1,0:T(8,128)(2,1)}, u32[]{:S(2)}, u32[]{:S(2)}) async-start(bf16[64,32,1024]{2,1,0:T(8,128)(2,1)} %bitcast.47), calls=%async_computation.2 | async-start | bytes 8388608 | tf_op jit(solution)/shard_map/all_to_all | solution.py:78
where the time goes:
time: 305 us; the launch traced here: 304 us
  other arithmetic  78.5 us (26%)
  waiting for transfers between devices  76.1 us (25%)
  blocking collectives  50.5 us (17%)
  local copies, waits for them, and re-layouts  44.7 us (15%)
  matrix products  38.6 us (13%)
  starting transfers between devices  15.1 us (5%)
    all_to_all x1, waiting for transfers between devices, local(): lax.all_to_all(picked, 'idx', split_axis=0, concat_axis=0, tiled=True)  44.7 us
    all_to_all x1, waiting for transfers between devices, local(): lax.all_to_all(send_back, 'idx', split_axis=0, concat_axis=0, tiled=True)  31.4 us
    psum x1, blocking collectives, local(): grad_shard = lax.psum(scatter_rows(wanted, returned, shard_rows), 'enc')  30.4 us
    scatter-add x1, other arithmetic, scatter_rows(): jnp.zeros((shard_rows, feature_dim), jnp.float32).at[target]  21.8 us
    all_to_all x1, blocking collectives, local(): lax.all_to_all(request, 'idx', split_axis=0, concat_axis=0, tiled=True)  20.2 us
    another operation x3, other arithmetic  18.5 us
    dot_general x1, matrix products, group_terms(): grad_query = jnp.dot(weights, neg_rows, preferred_element_type=jnp.float32)  15.6 us
    gather x1, local copies, waits for them, and re-layouts, local(): picked = jnp.take(passages, jnp.maximum(wanted, 0).reshape(-1), axis=0)  13.7 us
  transfers between devices with their start and end apart: 2, of which 2 were waited for; matrix products, arithmetic and copies ran while one was open for 7% of the time, Pallas kernels for 0%

commit v1 on v0

v1 whole, which is shorter than its diff:
```python
import functools
import math

import jax
import jax.numpy as jnp
from jax import lax
from jax.experimental import pallas as pl
from jax.experimental.pallas import tpu as pltpu
from jax.sharding import PartitionSpec as P

LSCALE = 32
CAP = 32
LANES = 128
MESH = pl.DeviceIdType.MESH
NONE = -1e30


def flip(u, v):
    if isinstance(u, int):
        return 1 - v if u else v
    return u + v - 2 * u * v


def place_bits(c, j, n, group):
    low = int(math.log2(group))
    count = int(math.log2(n))
    p = [(j >> k) & 1 for k in range(low)]
    p += [lax.rem(lax.div(c, 1 << k), 2) for k in range(count - low)]
    if n != 64:
        return p
    t0, t1, b0, b1, a0, a1 = p
    return [t0, t1, flip(t0, a0), flip(t1, a1), flip(t0, b0), flip(t1, b1)]


def place_of(distance, n):
    if n != 64:
        return distance
    z, x, y = distance & 3, (distance >> 2) & 3, (distance >> 4) & 3
    return ((x ^ z) << 4) + ((y ^ z) << 2) + z


def iota(shape, dim):
    return lax.broadcasted_iota(jnp.int32, shape, dim)


def dot(a, b, dims=((1,), (0,))):
    return lax.dot_general(a, b, (dims, ((), ())), preferred_element_type=jnp.float32)


def turned(rows):
    m = rows.shape[0]
    if m < LANES:
        rows = jnp.concatenate([rows, jnp.zeros((LANES - m, LANES), rows.dtype)], axis=0)
    return rows.T


def request_table(ids, me, n, shard_rows):
    slots = ids.shape[1]
    shift = int(math.log2(shard_rows))
    live = ids >= 0
    place = place_of(jnp.bitwise_xor(lax.shift_right_arithmetic(ids, shift), me), n)
    place = jnp.where(live, place, -1)
    row = jnp.bitwise_and(ids, shard_rows - 1) + 1
    hot = iota((n, slots), 0) == place
    hot_f = jnp.where(hot, 1.0, 0.0)
    width = min(256, slots)
    before = jnp.where(
        iota((width, width), 0) < iota((width, width), 1), 1.0, 0.0
    ).astype(jnp.bfloat16)
    carry = jnp.zeros((n, 1), jnp.float32)
    ranks = []
    for at in range(0, slots, width):
        part = hot_f[:, at : at + width]
        ahead = dot(part.astype(jnp.bfloat16), before) + carry
        ranks.append(jnp.sum(part * ahead, axis=0, keepdims=True))
        carry = carry + jnp.sum(part, axis=1, keepdims=True)
    rank = jnp.concatenate(ranks, axis=1).astype(jnp.int32)
    of_rank = jnp.where(iota((LANES, slots), 0) == rank, 1.0, 0.0).astype(jnp.bfloat16)
    high = lax.shift_right_arithmetic(row, 6).astype(jnp.float32)
    low = jnp.bitwise_and(row, 63).astype(jnp.float32)
    values = jnp.concatenate([hot_f * high, hot_f * low], axis=0).astype(jnp.bfloat16)
    table = dot(values, of_rank, ((1,), (1,)))
    return (table[:n] * 64.0 + table[n:]).astype(jnp.int32) - 1


def slot_row(table, n):
    slots = n * CAP
    shifted = table + 1
    high = lax.shift_right_arithmetic(shifted, 6).astype(jnp.float32)
    low = jnp.bitwise_and(shifted, 63).astype(jnp.float32)
    parts = jnp.concatenate([high, low], axis=0).astype(jnp.bfloat16)
    lane = jnp.bitwise_and(iota((LANES, slots), 1), CAP - 1)
    spread = jnp.where(iota((LANES, slots), 0) == lane, 1.0, 0.0).astype(jnp.bfloat16)
    wide = dot(parts, spread)
    both = wide[:n] * 64.0 + wide[n:]
    mine = lax.shift_right_arithmetic(iota((n, slots), 1), 5) == iota((n, slots), 0)
    row = jnp.sum(jnp.where(mine, both, 0.0), axis=0, keepdims=True)
    return row.astype(jnp.int32) - 1


def kernel(
    n, group,
    ids_ref, q_hbm, pos_hbm, pas_hbm,
    loss_ref, gq_hbm, gp_hbm,
    q, pos, pas, send, got, ret, big, wt,
    req, want, wcol, bias, wrow, tops, sums, prow, crow,
    load_s, rq_s, rq_r, f_s, f_r, r_s, r_r, fw_s, fw_r, wx_s, wx_r, oq_s, op_s,
):
    me, core = lax.axis_index("idx"), lax.axis_index("enc")
    queries, depth = q.shape
    shard_rows = pas.shape[0]
    slots = n * CAP
    chunk = group * CAP
    chunks = n // group
    scale = 3.0 / math.sqrt(depth)
    factor = LSCALE * scale
    steps = [
        (1 << k) * (1 - 2 * lax.rem(lax.div(me, 1 << k), 2))
        for k in range(int(math.log2(n)))
    ]

    def partner(c, j):
        bits = place_bits(c, j, n, group)
        there = me
        for bit, step in zip(bits, steps):
            if isinstance(bit, int):
                there = there + step if bit else there
            else:
                there = there + bit * step
        return there

    def each(work):
        def body(c, carry):
            for j in range(group):
                p = c * group + j
                if j == 0:
                    @pl.when(c > 0)
                    def _():
                        work(p, partner(c, 0))
                else:
                    work(p, partner(c, j))
            return carry

        lax.fori_loop(0, chunks, body, 0)

    def of_chunk(c, work):
        for j in range(group):
            p = c * group + j
            if j == 0:
                @pl.when(c > 0)
                def _():
                    work(p, partner(c, 0))
            else:
                work(p, partner(c, j))

    def part(c):
        return pl.ds(pl.multiple_of(c * chunk, chunk), chunk)

    def rows_at(p):
        return pl.ds(pl.multiple_of(p * CAP, CAP), CAP)

    def ask(p, there):
        return pltpu.make_async_remote_copy(
            src_ref=req.at[p], dst_ref=want.at[p], send_sem=rq_s.at[p],
            recv_sem=rq_r.at[p], device_id=(there, core), device_id_type=MESH)

    def fetch(p, there):
        return pltpu.make_async_remote_copy(
            src_ref=send.at[rows_at(p)], dst_ref=got.at[rows_at(p)], send_sem=f_s.at[p],
            recv_sem=f_r.at[p], device_id=(there, core), device_id_type=MESH)

    def give(p, there):
        return pltpu.make_async_remote_copy(
            src_ref=send.at[rows_at(p)], dst_ref=ret.at[core, rows_at(p)], send_sem=r_s.at[p],
            recv_sem=r_r.at[p], device_id=(there, core), device_id_type=MESH)

    def pass_on(c, whose):
        return pltpu.make_async_remote_copy(
            src_ref=ret.at[whose, part(c)], dst_ref=ret.at[whose, part(c)],
            send_sem=fw_s.at[c], recv_sem=fw_r.at[c],
            device_id=(me, 1 - core), device_id_type=MESH)

    def pass_row(whose):
        return pltpu.make_async_remote_copy(
            src_ref=wrow.at[whose], dst_ref=wrow.at[whose], send_sem=wx_s, recv_sem=wx_r,
            device_id=(me, 1 - core), device_id_type=MESH)

    loads = [
        pltpu.make_async_copy(src, dst, load_s.at[k])
        for k, (src, dst) in enumerate([(pas_hbm, pas), (q_hbm, q), (pos_hbm, pos)])
    ]

    barrier = pltpu.get_barrier_semaphore()
    each(lambda p, there: pl.semaphore_signal(
        barrier, inc=1, device_id=(there, core), device_id_type=MESH))
    pl.semaphore_signal(barrier, inc=1, device_id=(me, 1 - core), device_id_type=MESH)
    for load in loads:
        load.start()
    table = request_table(ids_ref[...], me, n, shard_rows)
    for p in range(n):
        req[p] = table[p : p + 1]
    want[0] = table[0:1]
    pl.semaphore_wait(barrier, n)

    each(lambda p, there: ask(p, there).start())
    each(lambda p, there: ask(p, there).wait_recv())
    wanted = want[:, 0, :]
    wanted_t = turned(wanted)
    for p in range(n):
        wcol[p * CAP : (p + 1) * CAP, :] = jnp.broadcast_to(
            wanted_t[:CAP, p : p + 1], (CAP, LANES))

    loads[0].wait()

    def gather(c, carry):
        w = wcol[part(c), :]
        lane = iota((chunk, LANES), 1)
        hot = jnp.concatenate(
            [jnp.where(w == lane + k, 1.0, 0.0).astype(jnp.bfloat16)
             for k in range(0, shard_rows, LANES)], axis=1)
        send[part(c), :] = dot(hot, pas[...]).astype(jnp.bfloat16)
        of_chunk(c, lambda p, there: fetch(p, there).start())
        return carry

    lax.fori_loop(0, chunks, gather, 0)
    got[0:CAP, :] = send[0:CAP, :]

    wrow[core] = slot_row(wanted, n)
    pass_row(core).start()
    asked_t = turned(req[:, 0, :])
    for p in range(n):
        bias[p * CAP : (p + 1) * CAP, :] = jnp.broadcast_to(
            jnp.where(asked_t[:CAP, p : p + 1] >= 0, 0.0, NONE), (CAP, LANES))
    loads[1].wait()
    loads[2].wait()
    block = min(256, queries)

    def block_at(b):
        return pl.ds(pl.multiple_of(b * block, block), block)

    def positive(b, carry):
        both = q[block_at(b), :].astype(jnp.float32) * pos[block_at(b), :].astype(jnp.float32)
        total = both[:, :LANES]
        for k in range(LANES, depth, LANES):
            total = total + both[:, k : k + LANES]
        prow[:, block_at(b)] = scale * jnp.sum(total.T, axis=0, keepdims=True)
        return carry

    lax.fori_loop(0, queries // block, positive, 0)

    wide = min(512, queries)

    def logits(c, carry):
        of_chunk(c, lambda p, there: fetch(p, there).wait_recv())

        def one(b, carry):
            at = pl.ds(pl.multiple_of(b * wide, wide), wide)
            x = scale * dot(got[part(c), :], q[at, :], ((1,), (1,)))
            x = x + jnp.concatenate([bias[part(c), :]] * (wide // LANES), axis=1)
            top = jnp.max(x, axis=0, keepdims=True)
            x = jnp.exp(x - top)
            big[part(c), at] = x
            tops[c, :, at] = top
            sums[c, :, at] = jnp.sum(x, axis=0, keepdims=True)
            return carry

        return lax.fori_loop(0, queries // wide, one, carry)

    lax.fori_loop(0, chunks, logits, 0)

    pos_logit = prow[...]
    top = pos_logit
    for c in range(chunks):
        top = jnp.maximum(top, tops[c])
    pos_exp = jnp.exp(pos_logit - top)
    total = pos_exp
    for c in range(chunks):
        total = total + sums[c] * jnp.exp(tops[c] - top)
    for c in range(chunks):
        tops[c] = jnp.exp(tops[c] - top) * (factor / total)
    crow[...] = factor * (pos_exp / total - 1.0)
    loss_ref[...] = top + jnp.log(total) - pos_logit

    each(lambda p, there: fetch(p, there).wait_send())

    def row_grads(c, carry):
        wt[part(c), :] = (big[part(c), :] * tops[c]).astype(jnp.bfloat16)
        send[part(c), :] = dot(wt[part(c), :], q[...]).astype(jnp.bfloat16)
        of_chunk(c, lambda p, there: give(p, there).start())
        return carry

    lax.fori_loop(0, chunks, row_grads, 0)
    ret[core, 0:CAP, :] = send[0:CAP, :]

    def out_q(b):
        return pltpu.make_async_copy(
            pas.at[block_at(b)], gq_hbm.at[block_at(b)], oq_s.at[b])

    def query_grads(b, carry):
        g = dot(wt[:, block_at(b)], got[...], ((0,), (0,)))
        coef = jnp.broadcast_to(crow[:, block_at(b)], (LANES, block)).T
        coef = jnp.concatenate([coef] * (depth // LANES), axis=1)
        g = g + coef * pos[block_at(b), :].astype(jnp.float32)
        pas[block_at(b), :] = g.astype(jnp.bfloat16)
        out_q(b).start()
        return carry

    lax.fori_loop(0, queries // block, query_grads, 0)

    tall = min(512, shard_rows)

    def tall_at(b):
        return pl.ds(pl.multiple_of(b * tall, tall), tall)

    def clear(b, carry):
        big[tall_at(b), 0:depth] = jnp.zeros((tall, depth), jnp.float32)
        return carry

    lax.fori_loop(0, shard_rows // tall, clear, 0)
    pass_row(1 - core).wait_recv()

    def collect(c, carry):
        @pl.when(c < chunks)
        def _():
            of_chunk(c, lambda p, there: give(p, there).wait_recv())
            pass_on(c, core).start()

        @pl.when(c > 0)
        def _():
            last = c - 1
            pass_on(last, 1 - core).wait_recv()

            def one(b, carry):
                here = iota((tall, chunk), 0) + b * tall
                total = big[tall_at(b), 0:depth]
                for whose in range(2):
                    hot = jnp.where(here == wrow[whose, :, part(last)], 1.0, 0.0)
                    total = total + dot(hot.astype(jnp.bfloat16), ret[whose, part(last), :])
                big[tall_at(b), 0:depth] = total
                return carry

            lax.fori_loop(0, shard_rows // tall, one, 0)

        return carry

    lax.fori_loop(0, chunks + 1, collect, 0)

    def out_p(b):
        return pltpu.make_async_copy(
            got.at[tall_at(b)], gp_hbm.at[tall_at(b)], op_s.at[b])

    def finish(b, carry):
        got[tall_at(b), :] = big[tall_at(b), 0:depth].astype(jnp.bfloat16)
        out_p(b).start()
        return carry

    lax.fori_loop(0, shard_rows // tall, finish, 0)

    each(lambda p, there: ask(p, there).wait_send())
    each(lambda p, there: give(p, there).wait_send())
    pass_row(core).wait_send()

    def close_pass(c, carry):
        pass_on(c, core).wait_send()
        return carry

    lax.fori_loop(0, chunks, close_pass, 0)

    def close_q(b, carry):
        out_q(b).wait()
        return carry

    lax.fori_loop(0, queries // block, close_q, 0)

    def close_p(b, carry):
        out_p(b).wait()
        return carry

    lax.fori_loop(0, shard_rows // tall, close_p, 0)


def local(group, queries, positives, passages, negatives):
    n = lax.axis_size("idx")
    count, depth = queries.shape
    shard_rows = passages.shape[0]
    slots = n * CAP
    chunks = n // group
    block = min(256, count)
    tall = min(512, shard_rows)
    any_space = pl.BlockSpec(memory_space=pl.ANY)
    vmem = pl.BlockSpec(memory_space=pltpu.VMEM)
    dma = pltpu.SemaphoreType.DMA
    bf16, f32 = jnp.bfloat16, jnp.float32
    loss, grad_q, grad_p = pl.pallas_call(
        functools.partial(kernel, n, group),
        out_shape=(
            jax.ShapeDtypeStruct((1, count), f32),
            jax.ShapeDtypeStruct((count, depth), bf16),
            jax.ShapeDtypeStruct((shard_rows, depth), bf16),
        ),
        in_specs=[vmem, any_space, any_space, any_space],
        out_specs=(vmem, any_space, any_space),
        scratch_shapes=[
            pltpu.VMEM((count, depth), bf16),
            pltpu.VMEM((count, depth), bf16),
            pltpu.VMEM((shard_rows, depth), bf16),
            pltpu.VMEM((slots, depth), bf16),
            pltpu.VMEM((slots, depth), bf16),
            pltpu.VMEM((2, slots, depth), bf16),
            pltpu.VMEM((slots, count), f32),
            pltpu.VMEM((slots, count), bf16),
            pltpu.VMEM((n, 1, LANES), jnp.int32),
            pltpu.VMEM((n, 1, LANES), jnp.int32),
            pltpu.VMEM((slots, LANES), jnp.int32),
            pltpu.VMEM((slots, LANES), f32),
            pltpu.VMEM((2, 1, slots), jnp.int32),
            pltpu.VMEM((chunks, 1, count), f32),
            pltpu.VMEM((chunks, 1, count), f32),
            pltpu.VMEM((1, count), f32),
            pltpu.VMEM((1, count), f32),
            dma((3,)),
            dma((n,)), dma((n,)),
            dma((n,)), dma((n,)),
            dma((n,)), dma((n,)),
            dma((chunks,)), dma((chunks,)),
            dma, dma,
            dma((count // block,)),
            dma((shard_rows // tall,)),
        ],
        compiler_params=pltpu.CompilerParams(
            collective_id=0, has_side_effects=True, vmem_limit_bytes=62 << 20
        ),
        cost_estimate=pl.CostEstimate(
            flops=12 * slots * count * depth, bytes_accessed=20 * count * depth,
            transcendentals=slots * count,
        ),
    )(negatives.reshape(1, -1), queries, positives, passages)
    return loss.reshape(-1), grad_q, grad_p


def solution(mesh, group=8):
    placed = (
        P(("idx", "enc"), None),
        P(("idx", "enc"), None),
        P("idx", None),
        P(("idx", "enc"), None),
    )
    return jax.shard_map(
        functools.partial(local, group),
        mesh=mesh,
        in_specs=placed,
        out_specs=(P(("idx", "enc")), P(("idx", "enc"), None), P("idx", None)),
        check_vma=False,
    )
```

time: 305 us -> 160 us (0.52)
  the two profiles are of different devices: /device:TPU:1 before, /device:TPU:56 now
where the time goes in v1:
time: 160 us
  Pallas kernels  151 us (94%)
  local copies, waits for them, and re-layouts  8.13 us (5%)
    pallas_call x1, Pallas kernels, local(): pl.pallas_call(functools.partial(kernel, n, group), out_shape=(jax.ShapeD...  151 us
    unnamed x5, local copies, waits for them, and re-layouts  8.13 us

profile of v1, /device:TPU:56, one launch (start us, length us, event | category | flops | bytes accessed | tf_op | source)
XLA Modules:
  0.0 160.2 jit_solution(15897206968803728076)
XLA Ops:
  0.6 151.5 %shard_map.67 = (f32[1,2048]{1,0:T(1,128)}, bf16[2048,1024]{1,0:T(8,128)(2,1)}, bf16[2048,1024]{1,0:T(8,128)(2,1)}) custom-call(s32[1,2048]{1,0:T(1,128)} %ids_ref.1, bf16[2048,1024]{1,0:T(8,128)(2,1)} %q_hbm.1, bf16[2048,1024]{1,0:T(8,128)(2,1)} %pos_hbm.1, bf16[2048,1024]{1,0:T(8,128)(2,1)} %pas_hbm.1), custom_call_target="tpu_custom_call" | custom-call | flops 51539607552 | bytes 41943040 | tf_op jit(solution)/shard_map/pallas_call | solution.py:394
  152.1 1.3 copy.10
  153.4 0.0 copy-start
  153.4 4.8 %copy.11 = bf16[2048,1024]{1,0:T(8,128)(2,1)} copy(bf16[2048,1024]{1,0:T(8,128)(2,1)} %get-tuple-element.13) | data formatting | bytes 8388608
  158.2 0.0 copy-done
  158.2 2.0 %copy.12 = bf16[2048,1024]{1,0:T(8,128)(2,1)} copy(bf16[2048,1024]{1,0:T(8,128)(2,1)S(1)} %copy-done) | data formatting | bytes 8388608
Async XLA Ops:
  153.4 4.8 %copy-start = (bf16[2048,1024]{1,0:T(8,128)(2,1)S(1)}, bf16[2048,1024]{1,0:T(8,128)(2,1)}, u32[]{:S(2)}) copy-start(bf16[2048,1024]{1,0:T(8,128)(2,1)} %get-tuple-element.14) | copy-start | bytes 12582916

commit v2 on v1

--- a/solution.py
+++ b/solution.py
@@ -24,8 +24,8 @@
 def place_bits(c, j, n, group):
     low = int(math.log2(group))
     count = int(math.log2(n))
-    p = [(j >> k) & 1 for k in range(low)]
-    p += [lax.rem(lax.div(c, 1 << k), 2) for k in range(count - low)]
+    p = [1 - ((j >> k) & 1) for k in range(low)]
+    p += [1 - lax.rem(lax.div(c, 1 << k), 2) for k in range(count - low)]
     if n != 64:
         return p
     t0, t1, b0, b1, a0, a1 = p
@@ -34,9 +34,9 @@
 
 def place_of(distance, n):
     if n != 64:
-        return distance
+        return n - 1 - distance
     z, x, y = distance & 3, (distance >> 2) & 3, (distance >> 4) & 3
-    return ((x ^ z) << 4) + ((y ^ z) << 2) + z
+    return n - 1 - (((x ^ z) << 4) + ((y ^ z) << 2) + z)
 
 
 def iota(shape, dim):
@@ -129,35 +129,40 @@
                 there = there + bit * step
         return there
 
-    def each(work):
-        def body(c, carry):
-            for j in range(group):
-                p = c * group + j
-                if j == 0:
-                    @pl.when(c > 0)
-                    def _():
-                        work(p, partner(c, 0))
-                else:
-                    work(p, partner(c, j))
-            return carry
-
-        lax.fori_loop(0, chunks, body, 0)
-
     def of_chunk(c, work):
         for j in range(group):
-            p = c * group + j
-            if j == 0:
-                @pl.when(c > 0)
+            if j == group - 1:
+                @pl.when(c < chunks - 1)
                 def _():
-                    work(p, partner(c, 0))
+                    work(c * group + j, partner(c, j))
             else:
-                work(p, partner(c, j))
+                work(c * group + j, partner(c, j))
+
+    def loop(start, stop, body):
+        def step(c, carry):
+            body(c)
+            return carry
+
+        lax.fori_loop(start, stop, step, 0)
+
+    def each(work):
+        loop(0, chunks, lambda c: of_chunk(c, work))
 
     def part(c):
         return pl.ds(pl.multiple_of(c * chunk, chunk), chunk)
 
     def rows_at(p):
         return pl.ds(pl.multiple_of(p * CAP, CAP), CAP)
+
+    def pair(c):
+        return pl.ds(pl.multiple_of(c * 2 * chunk, 2 * chunk), 2 * chunk)
+
+    def half(c, whose):
+        return pl.ds(pl.multiple_of((c * 2 + whose) * chunk, chunk), chunk)
+
+    def home(p, whose):
+        c, j = lax.div(p, group), lax.rem(p, group)
+        return pl.ds(pl.multiple_of((c * 2 + whose) * chunk + j * CAP, CAP), CAP)
 
     def ask(p, there):
         return pltpu.make_async_remote_copy(
@@ -171,12 +176,12 @@
 
     def give(p, there):
         return pltpu.make_async_remote_copy(
-            src_ref=send.at[rows_at(p)], dst_ref=ret.at[core, rows_at(p)], send_sem=r_s.at[p],
+            src_ref=send.at[rows_at(p)], dst_ref=ret.at[home(p, core)], send_sem=r_s.at[p],
             recv_sem=r_r.at[p], device_id=(there, core), device_id_type=MESH)
 
     def pass_on(c, whose):
         return pltpu.make_async_remote_copy(
-            src_ref=ret.at[whose, part(c)], dst_ref=ret.at[whose, part(c)],
+            src_ref=ret.at[half(c, whose)], dst_ref=ret.at[half(c, whose)],
             send_sem=fw_s.at[c], recv_sem=fw_r.at[c],
             device_id=(me, 1 - core), device_id_type=MESH)
 
@@ -199,184 +204,205 @@
     table = request_table(ids_ref[...], me, n, shard_rows)
     for p in range(n):
         req[p] = table[p : p + 1]
-    want[0] = table[0:1]
+    want[n - 1] = table[n - 1 : n]
     pl.semaphore_wait(barrier, n)
 
     each(lambda p, there: ask(p, there).start())
     each(lambda p, there: ask(p, there).wait_recv())
+
+    def columns(rows, into, change):
+        rows_t = turned(rows)
+        for p in range(n):
+            into[p * CAP : (p + 1) * CAP, :] = jnp.broadcast_to(
+                change(rows_t[:CAP, p : p + 1]), (CAP, LANES))
+
     wanted = want[:, 0, :]
-    wanted_t = turned(wanted)
-    for p in range(n):
-        wcol[p * CAP : (p + 1) * CAP, :] = jnp.broadcast_to(
-            wanted_t[:CAP, p : p + 1], (CAP, LANES))
+    columns(wanted, wcol, lambda x: x)
 
     loads[0].wait()
 
-    def gather(c, carry):
+    def gather(c):
         w = wcol[part(c), :]
         lane = iota((chunk, LANES), 1)
         hot = jnp.concatenate(
             [jnp.where(w == lane + k, 1.0, 0.0).astype(jnp.bfloat16)
              for k in range(0, shard_rows, LANES)], axis=1)
         send[part(c), :] = dot(hot, pas[...]).astype(jnp.bfloat16)
+
+    def gather_and_send(c):
+        gather(c)
         of_chunk(c, lambda p, there: fetch(p, there).start())
-        return carry
-
-    lax.fori_loop(0, chunks, gather, 0)
-    got[0:CAP, :] = send[0:CAP, :]
-
-    wrow[core] = slot_row(wanted, n)
-    pass_row(core).start()
-    asked_t = turned(req[:, 0, :])
-    for p in range(n):
-        bias[p * CAP : (p + 1) * CAP, :] = jnp.broadcast_to(
-            jnp.where(asked_t[:CAP, p : p + 1] >= 0, 0.0, NONE), (CAP, LANES))
-    loads[1].wait()
-    loads[2].wait()
+
+    ahead = min(4, chunks)
+    loop(0, ahead, gather_and_send)
+
     block = min(256, queries)
+    wide = min(512, queries)
 
     def block_at(b):
         return pl.ds(pl.multiple_of(b * block, block), block)
 
-    def positive(b, carry):
+    def other_form():
+        wrow[core] = slot_row(wanted, n)
+
+    def mask():
+        columns(req[:, 0, :], bias, lambda x: jnp.where(x >= 0, 0.0, NONE))
+
+    def positive(b):
         both = q[block_at(b), :].astype(jnp.float32) * pos[block_at(b), :].astype(jnp.float32)
         total = both[:, :LANES]
         for k in range(LANES, depth, LANES):
             total = total + both[:, k : k + LANES]
         prow[:, block_at(b)] = scale * jnp.sum(total.T, axis=0, keepdims=True)
-        return carry
-
-    lax.fori_loop(0, queries // block, positive, 0)
-
-    wide = min(512, queries)
-
-    def logits(c, carry):
-        of_chunk(c, lambda p, there: fetch(p, there).wait_recv())
-
-        def one(b, carry):
+
+    def turn(b):
+        wt[0:depth, block_at(b)] = q[block_at(b), :].T
+
+    other_form()
+    pass_row(core).start()
+    mask()
+    loads[1].wait()
+    loads[2].wait()
+    loop(0, queries // block, positive)
+    loop(0, queries // block, turn)
+
+    def logits(c):
+        def one(b):
             at = pl.ds(pl.multiple_of(b * wide, wide), wide)
-            x = scale * dot(got[part(c), :], q[at, :], ((1,), (1,)))
+            x = scale * dot(got[part(c), :], wt[0:depth, at])
             x = x + jnp.concatenate([bias[part(c), :]] * (wide // LANES), axis=1)
             top = jnp.max(x, axis=0, keepdims=True)
             x = jnp.exp(x - top)
             big[part(c), at] = x
             tops[c, :, at] = top
             sums[c, :, at] = jnp.sum(x, axis=0, keepdims=True)
-            return carry
-
-        return lax.fori_loop(0, queries // wide, one, carry)
-
-    lax.fori_loop(0, chunks, logits, 0)
-
-    pos_logit = prow[...]
-    top = pos_logit
-    for c in range(chunks):
-        top = jnp.maximum(top, tops[c])
-    pos_exp = jnp.exp(pos_logit - top)
-    total = pos_exp
-    for c in range(chunks):
-        total = total + sums[c] * jnp.exp(tops[c] - top)
-    for c in range(chunks):
-        tops[c] = jnp.exp(tops[c] - top) * (factor / total)
-    crow[...] = factor * (pos_exp / total - 1.0)
-    loss_ref[...] = top + jnp.log(total) - pos_logit
-
-    each(lambda p, there: fetch(p, there).wait_send())
-
-    def row_grads(c, carry):
+
+        loop(0, queries // wide, one)
+
+    def receive(c):
+        of_chunk(c, lambda p, there: fetch(p, there).wait_recv())
+
+        @pl.when(c == chunks - 1)
+        def _():
+            got[slots - CAP : slots, :] = send[slots - CAP : slots, :]
+
+        logits(c)
+
+    def gather_or_receive(c):
+        of_chunk(c - ahead, lambda p, there: fetch(p, there).wait_send())
+        gather_and_send(c)
+        receive(c - ahead)
+
+    loop(ahead, chunks, gather_or_receive)
+    loop(chunks - ahead, chunks, receive)
+
+    def totals():
+        pos_logit = prow[...]
+        top = pos_logit
+        for c in range(chunks):
+            top = jnp.maximum(top, tops[c])
+        pos_exp = jnp.exp(pos_logit - top)
+        total = pos_exp
+        for c in range(chunks):
+            total = total + sums[c] * jnp.exp(tops[c] - top)
+        for c in range(chunks):
+            tops[c] = jnp.exp(tops[c] - top) * (factor / total)
+        crow[...] = factor * (pos_exp / total - 1.0)
+        loss_ref[...] = top + jnp.log(total) - pos_logit
+
+    totals()
+
+    loop(chunks - ahead, chunks,
+         lambda c: of_chunk(c, lambda p, there: fetch(p, there).wait_send()))
+
+    def row_grads(c):
         wt[part(c), :] = (big[part(c), :] * tops[c]).astype(jnp.bfloat16)
         send[part(c), :] = dot(wt[part(c), :], q[...]).astype(jnp.bfloat16)
+
+    def return_rows(c):
+        row_grads(c)
         of_chunk(c, lambda p, there: give(p, there).start())
-        return carry
-
-    lax.fori_loop(0, chunks, row_grads, 0)
-    ret[core, 0:CAP, :] = send[0:CAP, :]
 
     def out_q(b):
         return pltpu.make_async_copy(
             pas.at[block_at(b)], gq_hbm.at[block_at(b)], oq_s.at[b])
 
-    def query_grads(b, carry):
+    def query_grads(b):
         g = dot(wt[:, block_at(b)], got[...], ((0,), (0,)))
         coef = jnp.broadcast_to(crow[:, block_at(b)], (LANES, block)).T
         coef = jnp.concatenate([coef] * (depth // LANES), axis=1)
         g = g + coef * pos[block_at(b), :].astype(jnp.float32)
         pas[block_at(b), :] = g.astype(jnp.bfloat16)
+
+    def query_grads_out(b):
+        query_grads(b)
         out_q(b).start()
-        return carry
-
-    lax.fori_loop(0, queries // block, query_grads, 0)
 
     tall = min(512, shard_rows)
 
     def tall_at(b):
         return pl.ds(pl.multiple_of(b * tall, tall), tall)
 
-    def clear(b, carry):
+    def clear(b):
         big[tall_at(b), 0:depth] = jnp.zeros((tall, depth), jnp.float32)
-        return carry
-
-    lax.fori_loop(0, shard_rows // tall, clear, 0)
+
+    loop(0, ahead, return_rows)
+
+    def return_more(c):
+        of_chunk(c - ahead, lambda p, there: give(p, there).wait_send())
+        return_rows(c)
+
+    loop(ahead, chunks, return_more)
+    ret[home(n - 1, core), :] = send[slots - CAP : slots, :]
+    loop(0, queries // block, query_grads_out)
+    loop(0, shard_rows // tall, clear)
     pass_row(1 - core).wait_recv()
-
-    def collect(c, carry):
-        @pl.when(c < chunks)
-        def _():
-            of_chunk(c, lambda p, there: give(p, there).wait_recv())
-            pass_on(c, core).start()
-
-        @pl.when(c > 0)
-        def _():
-            last = c - 1
-            pass_on(last, 1 - core).wait_recv()
-
-            def one(b, carry):
-                here = iota((tall, chunk), 0) + b * tall
-                total = big[tall_at(b), 0:depth]
-                for whose in range(2):
-                    hot = jnp.where(here == wrow[whose, :, part(last)], 1.0, 0.0)
-                    total = total + dot(hot.astype(jnp.bfloat16), ret[whose, part(last), :])
-                big[tall_at(b), 0:depth] = total
-                return carry
-
-            lax.fori_loop(0, shard_rows // tall, one, 0)
-
-        return carry
-
-    lax.fori_loop(0, chunks + 1, collect, 0)
 
     def out_p(b):
         return pltpu.make_async_copy(
             got.at[tall_at(b)], gp_hbm.at[tall_at(b)], op_s.at[b])
 
-    def finish(b, carry):
-        got[tall_at(b), :] = big[tall_at(b), 0:depth].astype(jnp.bfloat16)
+    def added(c, b):
+        here = iota((tall, chunk), 0) + b * tall
+        hot = jnp.concatenate(
+            [jnp.where(here == wrow[whose, :, part(c)], 1.0, 0.0).astype(jnp.bfloat16)
+             for whose in range(2)], axis=1)
+        return big[tall_at(b), 0:depth] + dot(hot, ret[pair(c), :])
+
+    def add_up(c):
+        def one(b):
+            big[tall_at(b), 0:depth] = added(c, b)
+
+        loop(0, shard_rows // tall, one)
+
+    def add_last(b):
+        got[tall_at(b), :] = added(chunks - 1, b).astype(jnp.bfloat16)
+
+    def add_last_out(b):
+        add_last(b)
         out_p(b).start()
-        return carry
-
-    lax.fori_loop(0, shard_rows // tall, finish, 0)
+
+    def take(c):
+        of_chunk(c, lambda p, there: give(p, there).wait_recv())
+        pass_on(c, core).start()
+
+    def collect(c):
+        take(c)
+        pass_on(c - 1, 1 - core).wait_recv()
+        add_up(c - 1)
+
+    take(0)
+    loop(1, chunks, collect)
+    pass_on(chunks - 1, 1 - core).wait_recv()
+    loop(0, shard_rows // tall, add_last_out)
 
     each(lambda p, there: ask(p, there).wait_send())
-    each(lambda p, there: give(p, there).wait_send())
+    loop(chunks - ahead, chunks,
+         lambda c: of_chunk(c, lambda p, there: give(p, there).wait_send()))
     pass_row(core).wait_send()
-
-    def close_pass(c, carry):
-        pass_on(c, core).wait_send()
-        return carry
-
-    lax.fori_loop(0, chunks, close_pass, 0)
-
-    def close_q(b, carry):
-        out_q(b).wait()
-        return carry
-
-    lax.fori_loop(0, queries // block, close_q, 0)
-
-    def close_p(b, carry):
-        out_p(b).wait()
-        return carry
-
-    lax.fori_loop(0, shard_rows // tall, close_p, 0)
+    loop(0, chunks, lambda c: pass_on(c, core).wait_send())
+    loop(0, queries // block, lambda b: out_q(b).wait())
+    loop(0, shard_rows // tall, lambda b: out_p(b).wait())
 
 
 def local(group, queries, positives, passages, negatives):
@@ -406,7 +432,7 @@
             pltpu.VMEM((shard_rows, depth), bf16),
             pltpu.VMEM((slots, depth), bf16),
             pltpu.VMEM((slots, depth), bf16),
-            pltpu.VMEM((2, slots, depth), bf16),
+            pltpu.VMEM((2 * slots, depth), bf16),
             pltpu.VMEM((slots, count), f32),
             pltpu.VMEM((slots, count), bf16),
             pltpu.VMEM((n, 1, LANES), jnp.int32),

time: 160 us -> 184 us (1.15)
  the two profiles are of different devices: /device:TPU:56 before, /device:TPU:13 now
where the time goes in v2:
time: 184 us
  Pallas kernels  175 us (95%)
  local copies, waits for them, and re-layouts  8.13 us (4%)
    pallas_call x1, Pallas kernels, local(): pl.pallas_call(functools.partial(kernel, n, group), out_shape=(jax.ShapeD...  175 us
    unnamed x5, local copies, waits for them, and re-layouts  8.13 us

profile of v2, /device:TPU:13, one launch (start us, length us, event | category | flops | bytes accessed | tf_op | source)
XLA Modules:
  0.0 183.7 jit_solution(5222153480706358194)
XLA Ops:
  0.6 174.9 %shard_map.67 = (f32[1,2048]{1,0:T(1,128)}, bf16[2048,1024]{1,0:T(8,128)(2,1)}, bf16[2048,1024]{1,0:T(8,128)(2,1)}) custom-call(s32[1,2048]{1,0:T(1,128)} %ids_ref.1, bf16[2048,1024]{1,0:T(8,128)(2,1)} %q_hbm.1, bf16[2048,1024]{1,0:T(8,128)(2,1)} %pos_hbm.1, bf16[2048,1024]{1,0:T(8,128)(2,1)} %pas_hbm.1), custom_call_target="tpu_custom_call" | custom-call | flops 51539607552 | bytes 41943040 | tf_op jit(solution)/shard_map/pallas_call | solution.py:420
  175.6 1.3 copy.10
  176.9 0.0 copy-start
  176.9 4.8 %copy.11 = bf16[2048,1024]{1,0:T(8,128)(2,1)} copy(bf16[2048,1024]{1,0:T(8,128)(2,1)} %get-tuple-element.13) | data formatting | bytes 8388608
  181.7 0.0 copy-done
  181.7 2.0 %copy.12 = bf16[2048,1024]{1,0:T(8,128)(2,1)} copy(bf16[2048,1024]{1,0:T(8,128)(2,1)S(1)} %copy-done) | data formatting | bytes 8388608
Async XLA Ops:
  176.9 4.8 %copy-start = (bf16[2048,1024]{1,0:T(8,128)(2,1)S(1)}, bf16[2048,1024]{1,0:T(8,128)(2,1)}, u32[]{:S(2)}) copy-start(bf16[2048,1024]{1,0:T(8,128)(2,1)} %get-tuple-element.14) | copy-start | bytes 12582916

commit v3 on v2

--- a/solution.py
+++ b/solution.py
@@ -101,10 +101,10 @@
 def kernel(
     n, group,
     ids_ref, q_hbm, pos_hbm, pas_hbm,
-    loss_ref, gq_hbm, gp_hbm,
-    q, pos, pas, send, got, ret, big, wt,
+    loss_ref, pas, pos,
+    q, send, got, ret, big, wt,
     req, want, wcol, bias, wrow, tops, sums, prow, crow,
-    load_s, rq_s, rq_r, f_s, f_r, r_s, r_r, fw_s, fw_r, wx_s, wx_r, oq_s, op_s,
+    load_s, rq_s, rq_r, f_s, f_r, r_s, r_r, fw_s, fw_r, wx_s, wx_r,
 ):
     me, core = lax.axis_index("idx"), lax.axis_index("enc")
     queries, depth = q.shape
@@ -233,7 +233,7 @@
         gather(c)
         of_chunk(c, lambda p, there: fetch(p, there).start())
 
-    ahead = min(4, chunks)
+    ahead = chunks
     loop(0, ahead, gather_and_send)
 
     block = min(256, queries)
@@ -323,10 +323,6 @@
         row_grads(c)
         of_chunk(c, lambda p, there: give(p, there).start())
 
-    def out_q(b):
-        return pltpu.make_async_copy(
-            pas.at[block_at(b)], gq_hbm.at[block_at(b)], oq_s.at[b])
-
     def query_grads(b):
         g = dot(wt[:, block_at(b)], got[...], ((0,), (0,)))
         coef = jnp.broadcast_to(crow[:, block_at(b)], (LANES, block)).T
@@ -334,10 +330,6 @@
         g = g + coef * pos[block_at(b), :].astype(jnp.float32)
         pas[block_at(b), :] = g.astype(jnp.bfloat16)
 
-    def query_grads_out(b):
-        query_grads(b)
-        out_q(b).start()
-
     tall = min(512, shard_rows)
 
     def tall_at(b):
@@ -354,13 +346,9 @@
 
     loop(ahead, chunks, return_more)
     ret[home(n - 1, core), :] = send[slots - CAP : slots, :]
-    loop(0, queries // block, query_grads_out)
+    loop(0, queries // block, query_grads)
     loop(0, shard_rows // tall, clear)
     pass_row(1 - core).wait_recv()
-
-    def out_p(b):
-        return pltpu.make_async_copy(
-            got.at[tall_at(b)], gp_hbm.at[tall_at(b)], op_s.at[b])
 
     def added(c, b):
         here = iota((tall, chunk), 0) + b * tall
@@ -376,11 +364,7 @@
         loop(0, shard_rows // tall, one)
 
     def add_last(b):
-        got[tall_at(b), :] = added(chunks - 1, b).astype(jnp.bfloat16)
-
-    def add_last_out(b):
-        add_last(b)
-        out_p(b).start()
+        pos[tall_at(b), :] = added(chunks - 1, b).astype(jnp.bfloat16)
 
     def take(c):
         of_chunk(c, lambda p, there: give(p, there).wait_recv())
@@ -394,15 +378,13 @@
     take(0)
     loop(1, chunks, collect)
     pass_on(chunks - 1, 1 - core).wait_recv()
-    loop(0, shard_rows // tall, add_last_out)
+    loop(0, shard_rows // tall, add_last)
 
     each(lambda p, there: ask(p, there).wait_send())
     loop(chunks - ahead, chunks,
          lambda c: of_chunk(c, lambda p, there: give(p, there).wait_send()))
     pass_row(core).wait_send()
     loop(0, chunks, lambda c: pass_on(c, core).wait_send())
-    loop(0, queries // block, lambda b: out_q(b).wait())
-    loop(0, shard_rows // tall, lambda b: out_p(b).wait())
 
 
 def local(group, queries, positives, passages, negatives):
@@ -411,8 +393,6 @@
     shard_rows = passages.shape[0]
     slots = n * CAP
     chunks = n // group
-    block = min(256, count)
-    tall = min(512, shard_rows)
     any_space = pl.BlockSpec(memory_space=pl.ANY)
     vmem = pl.BlockSpec(memory_space=pltpu.VMEM)
     dma = pltpu.SemaphoreType.DMA
@@ -421,15 +401,13 @@
         functools.partial(kernel, n, group),
         out_shape=(
             jax.ShapeDtypeStruct((1, count), f32),
-            jax.ShapeDtypeStruct((count, depth), bf16),
-            jax.ShapeDtypeStruct((shard_rows, depth), bf16),
+            pltpu.VMEM((count, depth), bf16),
+            pltpu.VMEM((shard_rows, depth), bf16),
         ),
         in_specs=[vmem, any_space, any_space, any_space],
-        out_specs=(vmem, any_space, any_space),
+        out_specs=(vmem, vmem, vmem),
         scratch_shapes=[
             pltpu.VMEM((count, depth), bf16),
-            pltpu.VMEM((count, depth), bf16),
-            pltpu.VMEM((shard_rows, depth), bf16),
             pltpu.VMEM((slots, depth), bf16),
             pltpu.VMEM((slots, depth), bf16),
             pltpu.VMEM((2 * slots, depth), bf16),
@@ -450,11 +428,9 @@
             dma((n,)), dma((n,)),
             dma((chunks,)), dma((chunks,)),
             dma, dma,
-            dma((count // block,)),
-            dma((shard_rows // tall,)),
         ],
         compiler_params=pltpu.CompilerParams(
-            collective_id=0, has_side_effects=True, vmem_limit_bytes=62 << 20
+            collective_id=0, has_side_effects=True, vmem_limit_bytes=52 << 20
         ),
         cost_estimate=pl.CostEstimate(
             flops=12 * slots * count * depth, bytes_accessed=20 * count * depth,

time: 184 us -> 155 us (0.84)
  the two profiles are of different devices: /device:TPU:13 before, /device:TPU:1 now
where the time goes in v3:
time: 155 us
  Pallas kernels  150 us (97%)
  local copies, waits for them, and re-layouts  4.63 us (3%)
    pallas_call x1, Pallas kernels, local(): pl.pallas_call(functools.partial(kernel, n, group), out_shape=(jax.ShapeD...  150 us
    unnamed x5, local copies, waits for them, and re-layouts  4.63 us

profile of v3, /device:TPU:1, one launch (start us, length us, event | category | flops | bytes accessed | tf_op | source)
XLA Modules:
  0.0 155.2 jit_solution(10560703380382556720)
XLA Ops:
  0.6 150.0 %shard_map.67 = (f32[1,2048]{1,0:T(1,128)}, bf16[2048,1024]{1,0:T(8,128)(2,1)S(1)}, bf16[2048,1024]{1,0:T(8,128)(2,1)S(1)}) custom-call(s32[1,2048]{1,0:T(1,128)} %ids_ref.1, bf16[2048,1024]{1,0:T(8,128)(2,1)} %q_hbm.1, bf16[2048,1024]{1,0:T(8,128)(2,1)} %pos_hbm.1, bf16[2048,1024]{1,0:T(8,128)(2,1)} %pas_hbm.1), custom_call_target="tpu_custom_call" | custom-call | flops 51539607552 | bytes 41943040 | tf_op jit(solution)/shard_map/pallas_call | solution.py:400
  150.6 2.0 %copy.10 = bf16[2048,1024]{1,0:T(8,128)(2,1)} copy(bf16[2048,1024]{1,0:T(8,128)(2,1)S(1)} %get-tuple-element.10) | data formatting | bytes 8388608
  152.6 0.0 copy-start
  152.6 2.0 %copy.11 = bf16[2048,1024]{1,0:T(8,128)(2,1)} copy(bf16[2048,1024]{1,0:T(8,128)(2,1)S(1)} %get-tuple-element.11) | data formatting | bytes 8388608
  154.6 0.0 copy-done
  154.6 0.6 copy.12
Async XLA Ops:
  152.6 2.0 %copy-start = (f32[1,2048]{1,0:T(1,128)S(1)}, f32[1,2048]{1,0:T(1,128)}, u32[]{:S(2)}) copy-start(f32[1,2048]{1,0:T(1,128)} %get-tuple-element.6) | copy-start | bytes 24580

commit v4 on v3

--- a/solution.py
+++ b/solution.py
@@ -24,8 +24,8 @@
 def place_bits(c, j, n, group):
     low = int(math.log2(group))
     count = int(math.log2(n))
-    p = [1 - ((j >> k) & 1) for k in range(low)]
-    p += [1 - lax.rem(lax.div(c, 1 << k), 2) for k in range(count - low)]
+    p = [(j >> k) & 1 for k in range(low)]
+    p += [lax.rem(lax.div(c, 1 << k), 2) for k in range(count - low)]
     if n != 64:
         return p
     t0, t1, b0, b1, a0, a1 = p
@@ -34,9 +34,9 @@
 
 def place_of(distance, n):
     if n != 64:
-        return n - 1 - distance
+        return distance
     z, x, y = distance & 3, (distance >> 2) & 3, (distance >> 4) & 3
-    return n - 1 - (((x ^ z) << 4) + ((y ^ z) << 2) + z)
+    return ((x ^ z) << 4) + ((y ^ z) << 2) + z
 
 
 def iota(shape, dim):
@@ -104,7 +104,7 @@
     loss_ref, pas, pos,
     q, send, got, ret, big, wt,
     req, want, wcol, bias, wrow, tops, sums, prow, crow,
-    load_s, rq_s, rq_r, f_s, f_r, r_s, r_r, fw_s, fw_r, wx_s, wx_r,
+    load_s, rq_s, rq_r, f_s, f_r, r_s, r_r, wx_s, wx_r, sw_s, sw_r, free_s,
 ):
     me, core = lax.axis_index("idx"), lax.axis_index("enc")
     queries, depth = q.shape
@@ -114,6 +114,7 @@
     chunks = n // group
     scale = 3.0 / math.sqrt(depth)
     factor = LSCALE * scale
+    cut = depth // 2
     steps = [
         (1 << k) * (1 - 2 * lax.rem(lax.div(me, 1 << k), 2))
         for k in range(int(math.log2(n)))
@@ -131,8 +132,8 @@
 
     def of_chunk(c, work):
         for j in range(group):
-            if j == group - 1:
-                @pl.when(c < chunks - 1)
+            if j == 0:
+                @pl.when(c > 0)
                 def _():
                     work(c * group + j, partner(c, j))
             else:
@@ -157,9 +158,6 @@
     def pair(c):
         return pl.ds(pl.multiple_of(c * 2 * chunk, 2 * chunk), 2 * chunk)
 
-    def half(c, whose):
-        return pl.ds(pl.multiple_of((c * 2 + whose) * chunk, chunk), chunk)
-
     def home(p, whose):
         c, j = lax.div(p, group), lax.rem(p, group)
         return pl.ds(pl.multiple_of((c * 2 + whose) * chunk + j * CAP, CAP), CAP)
@@ -174,15 +172,16 @@
             src_ref=send.at[rows_at(p)], dst_ref=got.at[rows_at(p)], send_sem=f_s.at[p],
             recv_sem=f_r.at[p], device_id=(there, core), device_id_type=MESH)
 
-    def give(p, there):
-        return pltpu.make_async_remote_copy(
-            src_ref=send.at[rows_at(p)], dst_ref=ret.at[home(p, core)], send_sem=r_s.at[p],
-            recv_sem=r_r.at[p], device_id=(there, core), device_id_type=MESH)
-
-    def pass_on(c, whose):
-        return pltpu.make_async_remote_copy(
-            src_ref=ret.at[half(c, whose)], dst_ref=ret.at[half(c, whose)],
-            send_sem=fw_s.at[c], recv_sem=fw_r.at[c],
+    def give(p, there, side):
+        return pltpu.make_async_remote_copy(
+            src_ref=send.at[rows_at(p), pl.ds(pl.multiple_of(side * cut, cut), cut)],
+            dst_ref=ret.at[home(p, core)], send_sem=r_s.at[side, p],
+            recv_sem=r_r.at[core, p], device_id=(there, side), device_id_type=MESH)
+
+    def given(p, whose):
+        return pltpu.make_async_remote_copy(
+            src_ref=ret.at[home(p, whose)], dst_ref=ret.at[home(p, whose)],
+            send_sem=r_s.at[whose, p], recv_sem=r_r.at[whose, p],
             device_id=(me, 1 - core), device_id_type=MESH)
 
     def pass_row(whose):
@@ -204,7 +203,7 @@
     table = request_table(ids_ref[...], me, n, shard_rows)
     for p in range(n):
         req[p] = table[p : p + 1]
-    want[n - 1] = table[n - 1 : n]
+    want[0] = table[0:1]
     pl.semaphore_wait(barrier, n)
 
     each(lambda p, there: ask(p, there).start())
@@ -233,8 +232,8 @@
         gather(c)
         of_chunk(c, lambda p, there: fetch(p, there).start())
 
-    ahead = chunks
-    loop(0, ahead, gather_and_send)
+    loop(0, chunks, gather_and_send)
+    got[0:CAP, :] = send[0:CAP, :]
 
     block = min(256, queries)
     wide = min(512, queries)
@@ -266,35 +265,30 @@
     loop(0, queries // block, positive)
     loop(0, queries // block, turn)
 
+    power = scale * math.log2(math.e)
+
     def logits(c):
-        def one(b):
-            at = pl.ds(pl.multiple_of(b * wide, wide), wide)
-            x = scale * dot(got[part(c), :], wt[0:depth, at])
+        def product(at):
+            return dot(got[part(c), :], wt[0:depth, at : at + wide])
+
+        ahead = product(0)
+        for at in range(0, queries, wide):
+            x = ahead
+            if at + wide < queries:
+                ahead = product(at + wide)
             x = x + jnp.concatenate([bias[part(c), :]] * (wide // LANES), axis=1)
             top = jnp.max(x, axis=0, keepdims=True)
-            x = jnp.exp(x - top)
-            big[part(c), at] = x
-            tops[c, :, at] = top
-            sums[c, :, at] = jnp.sum(x, axis=0, keepdims=True)
-
-        loop(0, queries // wide, one)
+            x = jnp.exp2(power * (x - top))
+            big[part(c), at : at + wide] = x
+            tops[c, :, at : at + wide] = scale * top
+            sums[c, :, at : at + wide] = jnp.sum(x, axis=0, keepdims=True)
 
     def receive(c):
         of_chunk(c, lambda p, there: fetch(p, there).wait_recv())
 
-        @pl.when(c == chunks - 1)
-        def _():
-            got[slots - CAP : slots, :] = send[slots - CAP : slots, :]
-
         logits(c)
 
-    def gather_or_receive(c):
-        of_chunk(c - ahead, lambda p, there: fetch(p, there).wait_send())
-        gather_and_send(c)
-        receive(c - ahead)
-
-    loop(ahead, chunks, gather_or_receive)
-    loop(chunks - ahead, chunks, receive)
+    loop(0, chunks, receive)
 
     def totals():
         pos_logit = prow[...]
@@ -312,8 +306,7 @@
 
     totals()
 
-    loop(chunks - ahead, chunks,
-         lambda c: of_chunk(c, lambda p, there: fetch(p, there).wait_send()))
+    each(lambda p, there: fetch(p, there).wait_send())
 
     def row_grads(c):
         wt[part(c), :] = (big[part(c), :] * tops[c]).astype(jnp.bfloat16)
@@ -321,14 +314,26 @@
 
     def return_rows(c):
         row_grads(c)
-        of_chunk(c, lambda p, there: give(p, there).start())
+
+        @pl.when(c == 0)
+        def _():
+            give(0, me, 1 - core).start()
+
+        def both(p, there):
+            give(p, there, 0).start()
+            give(p, there, 1).start()
+
+        of_chunk(c, both)
+
+    def wide_at(b):
+        return pl.ds(pl.multiple_of(b * wide, wide), wide)
 
     def query_grads(b):
-        g = dot(wt[:, block_at(b)], got[...], ((0,), (0,)))
-        coef = jnp.broadcast_to(crow[:, block_at(b)], (LANES, block)).T
+        g = dot(wt[:, wide_at(b)], got[...], ((0,), (0,)))
+        coef = jnp.broadcast_to(crow[:, wide_at(b)], (LANES, wide)).T
         coef = jnp.concatenate([coef] * (depth // LANES), axis=1)
-        g = g + coef * pos[block_at(b), :].astype(jnp.float32)
-        pas[block_at(b), :] = g.astype(jnp.bfloat16)
+        g = g + coef * pos[wide_at(b), :].astype(jnp.float32)
+        pas[wide_at(b), :] = g.astype(jnp.bfloat16)
 
     tall = min(512, shard_rows)
 
@@ -336,17 +341,13 @@
         return pl.ds(pl.multiple_of(b * tall, tall), tall)
 
     def clear(b):
-        big[tall_at(b), 0:depth] = jnp.zeros((tall, depth), jnp.float32)
-
-    loop(0, ahead, return_rows)
-
-    def return_more(c):
-        of_chunk(c - ahead, lambda p, there: give(p, there).wait_send())
-        return_rows(c)
-
-    loop(ahead, chunks, return_more)
-    ret[home(n - 1, core), :] = send[slots - CAP : slots, :]
-    loop(0, queries // block, query_grads)
+        big[tall_at(b), 0:cut] = jnp.zeros((tall, cut), jnp.float32)
+
+    loop(0, chunks, return_rows)
+    mine = pl.ds(pl.multiple_of(core * cut, cut), cut)
+    ret[home(0, core), :] = send[0:CAP, mine]
+    loop(0, queries // wide, query_grads)
+    pl.semaphore_signal(free_s, inc=1, device_id=(me, 1 - core), device_id_type=MESH)
     loop(0, shard_rows // tall, clear)
     pass_row(1 - core).wait_recv()
 
@@ -355,36 +356,52 @@
         hot = jnp.concatenate(
             [jnp.where(here == wrow[whose, :, part(c)], 1.0, 0.0).astype(jnp.bfloat16)
              for whose in range(2)], axis=1)
-        return big[tall_at(b), 0:depth] + dot(hot, ret[pair(c), :])
+        return big[tall_at(b), 0:cut] + dot(hot, ret[pair(c), :])
 
     def add_up(c):
-        def one(b):
-            big[tall_at(b), 0:depth] = added(c, b)
-
-        loop(0, shard_rows // tall, one)
+        for b in range(shard_rows // tall):
+            big[tall_at(b), 0:cut] = added(c, b)
 
     def add_last(b):
-        pos[tall_at(b), :] = added(chunks - 1, b).astype(jnp.bfloat16)
+        pos[tall_at(b), mine] = added(chunks - 1, b).astype(jnp.bfloat16)
+
+    def swap(b, side):
+        block = pos.at[tall_at(b), pl.ds(pl.multiple_of(side * cut, cut), cut)]
+        return pltpu.make_async_remote_copy(
+            src_ref=block, dst_ref=block, send_sem=sw_s.at[b], recv_sem=sw_r.at[b],
+            device_id=(me, 1 - core), device_id_type=MESH)
 
     def take(c):
-        of_chunk(c, lambda p, there: give(p, there).wait_recv())
-        pass_on(c, core).start()
+        def both(p, there):
+            given(p, 0).wait_recv()
+            given(p, 1).wait_recv()
+
+        of_chunk(c, both)
 
     def collect(c):
         take(c)
-        pass_on(c - 1, 1 - core).wait_recv()
-        add_up(c - 1)
-
-    take(0)
-    loop(1, chunks, collect)
-    pass_on(chunks - 1, 1 - core).wait_recv()
-    loop(0, shard_rows // tall, add_last)
+        add_up(c)
+
+    given(0, 1 - core).wait_recv()
+    loop(0, chunks - 1, collect)
+    take(chunks - 1)
+    pl.semaphore_wait(free_s, 1)
+    for b in range(shard_rows // tall):
+        add_last(b)
+        swap(b, core).start()
 
     each(lambda p, there: ask(p, there).wait_send())
-    loop(chunks - ahead, chunks,
-         lambda c: of_chunk(c, lambda p, there: give(p, there).wait_send()))
+
+    def sent(p, there):
+        give(p, there, 0).wait_send()
+        give(p, there, 1).wait_send()
+
+    each(sent)
+    give(0, me, 1 - core).wait_send()
     pass_row(core).wait_send()
-    loop(0, chunks, lambda c: pass_on(c, core).wait_send())
+    for b in range(shard_rows // tall):
+        swap(b, core).wait_send()
+        swap(b, 1 - core).wait_recv()
 
 
 def local(group, queries, positives, passages, negatives):
@@ -410,7 +427,7 @@
             pltpu.VMEM((count, depth), bf16),
             pltpu.VMEM((slots, depth), bf16),
             pltpu.VMEM((slots, depth), bf16),
-            pltpu.VMEM((2 * slots, depth), bf16),
+            pltpu.VMEM((2 * slots, depth // 2), bf16),
             pltpu.VMEM((slots, count), f32),
             pltpu.VMEM((slots, count), bf16),
             pltpu.VMEM((n, 1, LANES), jnp.int32),
@@ -425,9 +442,11 @@
             dma((3,)),
             dma((n,)), dma((n,)),
             dma((n,)), dma((n,)),
-            dma((n,)), dma((n,)),
-            dma((chunks,)), dma((chunks,)),
+            dma((2, n)), dma((2, n)),
             dma, dma,
+            dma((shard_rows // min(512, shard_rows),)),
+            dma((shard_rows // min(512, shard_rows),)),
+            pltpu.SemaphoreType.REGULAR,
         ],
         compiler_params=pltpu.CompilerParams(
             collective_id=0, has_side_effects=True, vmem_limit_bytes=52 << 20

time: 155 us -> 142 us (0.916)
  Pallas kernels: 150 us -> 136 us
    pallas_call x1, Pallas kernels: 150 us -> 136 us  [local(): pl.pallas_call(functools.partial(kernel, n, group), out_shape=(jax.ShapeD...]
where the time goes in v4:
time: 142 us
  Pallas kernels  136 us (96%)
  local copies, waits for them, and re-layouts  4.63 us (3%)
    pallas_call x1, Pallas kernels, local(): pl.pallas_call(functools.partial(kernel, n, group), out_shape=(jax.ShapeD...  136 us
    unnamed x5, local copies, waits for them, and re-layouts  4.63 us

profile of v4, /device:TPU:1, one launch (start us, length us, event | category | flops | bytes accessed | tf_op | source)
XLA Modules:
  0.0 141.7 jit_solution(15328737921724406215)
XLA Ops:
  0.6 136.4 %shard_map.67 = (f32[1,2048]{1,0:T(1,128)}, bf16[2048,1024]{1,0:T(8,128)(2,1)S(1)}, bf16[2048,1024]{1,0:T(8,128)(2,1)S(1)}) custom-call(s32[1,2048]{1,0:T(1,128)} %ids_ref.1, bf16[2048,1024]{1,0:T(8,128)(2,1)} %q_hbm.1, bf16[2048,1024]{1,0:T(8,128)(2,1)} %pos_hbm.1, bf16[2048,1024]{1,0:T(8,128)(2,1)} %pas_hbm.1), custom_call_target="tpu_custom_call" | custom-call | flops 51539607552 | bytes 41943040 | tf_op jit(solution)/shard_map/pallas_call | solution.py:417
  137.1 2.0 %copy.10 = bf16[2048,1024]{1,0:T(8,128)(2,1)} copy(bf16[2048,1024]{1,0:T(8,128)(2,1)S(1)} %get-tuple-element.10) | data formatting | bytes 8388608
  139.1 0.0 copy-start
  139.1 2.0 %copy.11 = bf16[2048,1024]{1,0:T(8,128)(2,1)} copy(bf16[2048,1024]{1,0:T(8,128)(2,1)S(1)} %get-tuple-element.11) | data formatting | bytes 8388608
  141.1 0.0 copy-done
  141.1 0.6 copy.12
Async XLA Ops:
  139.1 2.0 %copy-start = (f32[1,2048]{1,0:T(1,128)S(1)}, f32[1,2048]{1,0:T(1,128)}, u32[]{:S(2)}) copy-start(f32[1,2048]{1,0:T(1,128)} %get-tuple-element.6) | copy-start | bytes 24580

commit v5 on v4

--- a/solution.py
+++ b/solution.py
@@ -103,8 +103,8 @@
     ids_ref, q_hbm, pos_hbm, pas_hbm,
     loss_ref, pas, pos,
     q, send, got, ret, big, wt,
-    req, want, wcol, bias, wrow, tops, sums, prow, crow,
-    load_s, rq_s, rq_r, f_s, f_r, r_s, r_r, wx_s, wx_r, sw_s, sw_r, free_s,
+    req, want, bias, wrow, tops, sums, prow, crow,
+    load_s, rq_s, rq_r, f_s, f_r, r_s, r_r, wx_s, wx_r, sw_s, sw_r, free_s, near_s,
 ):
     me, core = lax.axis_index("idx"), lax.axis_index("enc")
     queries, depth = q.shape
@@ -195,8 +195,21 @@
     ]
 
     barrier = pltpu.get_barrier_semaphore()
-    each(lambda p, there: pl.semaphore_signal(
-        barrier, inc=1, device_id=(there, core), device_id_type=MESH))
+    axes = [steps[k : k + 2] for k in range(0, len(steps), 2)]
+
+    def along(axis):
+        return [
+            sum([s for k, s in enumerate(axis) if far >> k & 1], me)
+            for far in range(1, 1 << len(axis))
+        ]
+
+    def greet(semaphore, axis):
+        for there in along(axis):
+            pl.semaphore_signal(
+                semaphore, inc=1, device_id=(there, core), device_id_type=MESH)
+
+    for axis in axes:
+        greet(barrier, axis)
     pl.semaphore_signal(barrier, inc=1, device_id=(me, 1 - core), device_id_type=MESH)
     for load in loads:
         load.start()
@@ -204,10 +217,12 @@
     for p in range(n):
         req[p] = table[p : p + 1]
     want[0] = table[0:1]
-    pl.semaphore_wait(barrier, n)
+    pl.semaphore_wait(barrier, 1 + sum(len(along(axis)) for axis in axes))
+    for k, axis in enumerate(axes[1:]):
+        greet(near_s.at[k], axis)
+        pl.semaphore_wait(near_s.at[k], len(along(axis)))
 
     each(lambda p, there: ask(p, there).start())
-    each(lambda p, there: ask(p, there).wait_recv())
 
     def columns(rows, into, change):
         rows_t = turned(rows)
@@ -215,13 +230,13 @@
             into[p * CAP : (p + 1) * CAP, :] = jnp.broadcast_to(
                 change(rows_t[:CAP, p : p + 1]), (CAP, LANES))
 
-    wanted = want[:, 0, :]
-    columns(wanted, wcol, lambda x: x)
-
     loads[0].wait()
 
     def gather(c):
-        w = wcol[part(c), :]
+        asked = turned(want[pl.ds(c * group, group), 0, :])
+        w = jnp.concatenate(
+            [jnp.broadcast_to(asked[:CAP, j : j + 1], (CAP, LANES)) for j in range(group)],
+            axis=0)
         lane = iota((chunk, LANES), 1)
         hot = jnp.concatenate(
             [jnp.where(w == lane + k, 1.0, 0.0).astype(jnp.bfloat16)
@@ -229,6 +244,7 @@
         send[part(c), :] = dot(hot, pas[...]).astype(jnp.bfloat16)
 
     def gather_and_send(c):
+        of_chunk(c, lambda p, there: ask(p, there).wait_recv())
         gather(c)
         of_chunk(c, lambda p, there: fetch(p, there).start())
 
@@ -242,7 +258,7 @@
         return pl.ds(pl.multiple_of(b * block, block), block)
 
     def other_form():
-        wrow[core] = slot_row(wanted, n)
+        wrow[core] = slot_row(want[:, 0, :], n)
 
     def mask():
         columns(req[:, 0, :], bias, lambda x: jnp.where(x >= 0, 0.0, NONE))
@@ -264,6 +280,7 @@
     loads[2].wait()
     loop(0, queries // block, positive)
     loop(0, queries // block, turn)
+    each(lambda p, there: ask(p, there).wait_send())
 
     power = scale * math.log2(math.e)
 
@@ -306,13 +323,12 @@
 
     totals()
 
-    each(lambda p, there: fetch(p, there).wait_send())
-
     def row_grads(c):
         wt[part(c), :] = (big[part(c), :] * tops[c]).astype(jnp.bfloat16)
         send[part(c), :] = dot(wt[part(c), :], q[...]).astype(jnp.bfloat16)
 
     def return_rows(c):
+        of_chunk(c, lambda p, there: fetch(p, there).wait_send())
         row_grads(c)
 
         @pl.when(c == 0)
@@ -389,8 +405,6 @@
     for b in range(shard_rows // tall):
         add_last(b)
         swap(b, core).start()
-
-    each(lambda p, there: ask(p, there).wait_send())
 
     def sent(p, there):
         give(p, there, 0).wait_send()
@@ -432,7 +446,6 @@
             pltpu.VMEM((slots, count), bf16),
             pltpu.VMEM((n, 1, LANES), jnp.int32),
             pltpu.VMEM((n, 1, LANES), jnp.int32),
-            pltpu.VMEM((slots, LANES), jnp.int32),
             pltpu.VMEM((slots, LANES), f32),
             pltpu.VMEM((2, 1, slots), jnp.int32),
             pltpu.VMEM((chunks, 1, count), f32),
@@ -447,6 +460,7 @@
             dma((shard_rows // min(512, shard_rows),)),
             dma((shard_rows // min(512, shard_rows),)),
             pltpu.SemaphoreType.REGULAR,
+            pltpu.SemaphoreType.REGULAR((2,)),
         ],
         compiler_params=pltpu.CompilerParams(
             collective_id=0, has_side_effects=True, vmem_limit_bytes=52 << 20

time: 142 us -> 145 us (1.021)
  Pallas kernels: 136 us -> 139 us
    pallas_call x1, Pallas kernels: 136 us -> 139 us  [local(): pl.pallas_call(functools.partial(kernel, n, group), out_shape=(jax.ShapeD...]
where the time goes in v5:
time: 145 us
  Pallas kernels  139 us (96%)
  local copies, waits for them, and re-layouts  4.63 us (3%)
    pallas_call x1, Pallas kernels, local(): pl.pallas_call(functools.partial(kernel, n, group), out_shape=(jax.ShapeD...  139 us
    unnamed x5, local copies, waits for them, and re-layouts  4.63 us

profile of v5, /device:TPU:1, one launch (start us, length us, event | category | flops | bytes accessed | tf_op | source)
XLA Modules:
  0.0 144.7 jit_solution(566771276396634757)
XLA Ops:
  0.6 139.5 %shard_map.67 = (f32[1,2048]{1,0:T(1,128)}, bf16[2048,1024]{1,0:T(8,128)(2,1)S(1)}, bf16[2048,1024]{1,0:T(8,128)(2,1)S(1)}) custom-call(s32[1,2048]{1,0:T(1,128)} %ids_ref.1, bf16[2048,1024]{1,0:T(8,128)(2,1)} %q_hbm.1, bf16[2048,1024]{1,0:T(8,128)(2,1)} %pos_hbm.1, bf16[2048,1024]{1,0:T(8,128)(2,1)} %pas_hbm.1), custom_call_target="tpu_custom_call" | custom-call | flops 51539607552 | bytes 41943040 | tf_op jit(solution)/shard_map/pallas_call | solution.py:431
  140.1 2.0 %copy.10 = bf16[2048,1024]{1,0:T(8,128)(2,1)} copy(bf16[2048,1024]{1,0:T(8,128)(2,1)S(1)} %get-tuple-element.10) | data formatting | bytes 8388608
  142.1 0.0 copy-start
  142.1 2.0 %copy.11 = bf16[2048,1024]{1,0:T(8,128)(2,1)} copy(bf16[2048,1024]{1,0:T(8,128)(2,1)S(1)} %get-tuple-element.11) | data formatting | bytes 8388608
  144.1 0.0 copy-done
  144.1 0.6 copy.12
Async XLA Ops:
  142.1 2.0 %copy-start = (f32[1,2048]{1,0:T(1,128)S(1)}, f32[1,2048]{1,0:T(1,128)}, u32[]{:S(2)}) copy-start(f32[1,2048]{1,0:T(1,128)} %get-tuple-element.6) | copy-start | bytes 24580

commit v6 on v4

--- a/solution.py
+++ b/solution.py
@@ -103,7 +103,7 @@
     ids_ref, q_hbm, pos_hbm, pas_hbm,
     loss_ref, pas, pos,
     q, send, got, ret, big, wt,
-    req, want, wcol, bias, wrow, tops, sums, prow, crow,
+    req, want, bias, wrow, tops, sums, prow, crow,
     load_s, rq_s, rq_r, f_s, f_r, r_s, r_r, wx_s, wx_r, sw_s, sw_r, free_s,
 ):
     me, core = lax.axis_index("idx"), lax.axis_index("enc")
@@ -207,7 +207,6 @@
     pl.semaphore_wait(barrier, n)
 
     each(lambda p, there: ask(p, there).start())
-    each(lambda p, there: ask(p, there).wait_recv())
 
     def columns(rows, into, change):
         rows_t = turned(rows)
@@ -215,13 +214,13 @@
             into[p * CAP : (p + 1) * CAP, :] = jnp.broadcast_to(
                 change(rows_t[:CAP, p : p + 1]), (CAP, LANES))
 
-    wanted = want[:, 0, :]
-    columns(wanted, wcol, lambda x: x)
-
     loads[0].wait()
 
     def gather(c):
-        w = wcol[part(c), :]
+        asked = turned(want[pl.ds(c * group, group), 0, :])
+        w = jnp.concatenate(
+            [jnp.broadcast_to(asked[:CAP, j : j + 1], (CAP, LANES)) for j in range(group)],
+            axis=0)
         lane = iota((chunk, LANES), 1)
         hot = jnp.concatenate(
             [jnp.where(w == lane + k, 1.0, 0.0).astype(jnp.bfloat16)
@@ -229,6 +228,7 @@
         send[part(c), :] = dot(hot, pas[...]).astype(jnp.bfloat16)
 
     def gather_and_send(c):
+        of_chunk(c, lambda p, there: ask(p, there).wait_recv())
         gather(c)
         of_chunk(c, lambda p, there: fetch(p, there).start())
 
@@ -242,7 +242,7 @@
         return pl.ds(pl.multiple_of(b * block, block), block)
 
     def other_form():
-        wrow[core] = slot_row(wanted, n)
+        wrow[core] = slot_row(want[:, 0, :], n)
 
     def mask():
         columns(req[:, 0, :], bias, lambda x: jnp.where(x >= 0, 0.0, NONE))
@@ -264,6 +264,7 @@
     loads[2].wait()
     loop(0, queries // block, positive)
     loop(0, queries // block, turn)
+    each(lambda p, there: ask(p, there).wait_send())
 
     power = scale * math.log2(math.e)
 
@@ -306,13 +307,12 @@
 
     totals()
 
-    each(lambda p, there: fetch(p, there).wait_send())
-
     def row_grads(c):
         wt[part(c), :] = (big[part(c), :] * tops[c]).astype(jnp.bfloat16)
         send[part(c), :] = dot(wt[part(c), :], q[...]).astype(jnp.bfloat16)
 
     def return_rows(c):
+        of_chunk(c, lambda p, there: fetch(p, there).wait_send())
         row_grads(c)
 
         @pl.when(c == 0)
@@ -390,8 +390,6 @@
         add_last(b)
         swap(b, core).start()
 
-    each(lambda p, there: ask(p, there).wait_send())
-
     def sent(p, there):
         give(p, there, 0).wait_send()
         give(p, there, 1).wait_send()
@@ -402,6 +400,18 @@
     for b in range(shard_rows // tall):
         swap(b, core).wait_send()
         swap(b, 1 - core).wait_recv()
+
+
+def hand_over(loss, grad_q, grad_p, loss_out, grad_q_out, grad_p_out, done):
+    moves = [
+        pltpu.make_async_copy(src, dst, done.at[k])
+        for k, (src, dst) in enumerate(
+            [(grad_p, grad_p_out), (grad_q, grad_q_out), (loss, loss_out)])
+    ]
+    for move in moves:
+        move.start()
+    for move in moves:
+        move.wait()
 
 
 def local(group, queries, positives, passages, negatives):
@@ -417,7 +427,7 @@
     loss, grad_q, grad_p = pl.pallas_call(
         functools.partial(kernel, n, group),
         out_shape=(
-            jax.ShapeDtypeStruct((1, count), f32),
+            pltpu.VMEM((1, count), f32),
             pltpu.VMEM((count, depth), bf16),
             pltpu.VMEM((shard_rows, depth), bf16),
         ),
@@ -432,7 +442,6 @@
             pltpu.VMEM((slots, count), bf16),
             pltpu.VMEM((n, 1, LANES), jnp.int32),
             pltpu.VMEM((n, 1, LANES), jnp.int32),
-            pltpu.VMEM((slots, LANES), jnp.int32),
             pltpu.VMEM((slots, LANES), f32),
             pltpu.VMEM((2, 1, slots), jnp.int32),
             pltpu.VMEM((chunks, 1, count), f32),
@@ -456,6 +465,18 @@
             transcendentals=slots * count,
         ),
     )(negatives.reshape(1, -1), queries, positives, passages)
+    loss, grad_q, grad_p = pl.pallas_call(
+        hand_over,
+        out_shape=(
+            jax.ShapeDtypeStruct((1, count), f32),
+            jax.ShapeDtypeStruct((count, depth), bf16),
+            jax.ShapeDtypeStruct((shard_rows, depth), bf16),
+        ),
+        in_specs=[any_space] * 3,
+        out_specs=(any_space,) * 3,
+        scratch_shapes=[dma((3,))],
+        compiler_params=pltpu.CompilerParams(vmem_limit_bytes=1 << 20),
+    )(loss, grad_q, grad_p)
     return loss.reshape(-1), grad_q, grad_p
 
 

time: 142 us -> 141 us (level)
  local copies, waits for them, and re-layouts: 4.63 us -> 0 us
  Pallas kernels: 136 us -> 140 us
    unnamed x5 -> x0, local copies, waits for them, and re-layouts: 4.63 us -> none
    pallas_call x1 -> x2, Pallas kernels: 136 us -> 140 us  [the longest x1 137 us: local(): pl.pallas_call(functools.partial(kernel, n, group), out_shape=(pltpu.VMEM...]
where the time goes in v6:
time: 141 us
  Pallas kernels  140 us (99%)
    pallas_call x1, Pallas kernels, local(): pl.pallas_call(functools.partial(kernel, n, group), out_shape=(pltpu.VMEM...  137 us
    pallas_call x1, Pallas kernels, local(): pl.pallas_call(hand_over, out_shape=(jax.ShapeDtypeStruct((1, count), f32...  3.42 us

profile of v6, /device:TPU:1, one launch (start us, length us, event | category | flops | bytes accessed | tf_op | source)
XLA Modules:
  0.0 140.8 jit_solution(334586409007981482)
XLA Ops:
  0.6 136.8 %shard_map.67 = (f32[1,2048]{1,0:T(1,128)S(1)}, bf16[2048,1024]{1,0:T(8,128)(2,1)S(1)}, bf16[2048,1024]{1,0:T(8,128)(2,1)S(1)}) custom-call(s32[1,2048]{1,0:T(1,128)} %ids_ref.1, bf16[2048,1024]{1,0:T(8,128)(2,1)} %q_hbm.1, bf16[2048,1024]{1,0:T(8,128)(2,1)} %pos_hbm.1, bf16[2048,1024]{1,0:T(8,128)(2,1)} %pas_hbm.1), custom_call_target="tpu_custom_call" | custom-call | flops 51539607552 | bytes 41943040 | tf_op jit(solution)/shard_map/pallas_call | solution.py:427
  137.4 3.4 %shard_map.68 = (f32[1,2048]{1,0:T(1,128)}, bf16[2048,1024]{1,0:T(8,128)(2,1)}, bf16[2048,1024]{1,0:T(8,128)(2,1)}) custom-call(f32[1,2048]{1,0:T(1,128)S(1)} %get-tuple-element.9.loss, bf16[2048,1024]{1,0:T(8,128)(2,1)S(1)} %get-tuple-element.10.grad_q, bf16[2048,1024]{1,0:T(8,128)(2,1)S(1)} %get-tuple-element.11.grad_p), custom_call_target="tpu_custom_call" | custom-call | tf_op jit(solution)/shard_map/pallas_call | solution.py:468

commit v7 on v6

--- a/solution.py
+++ b/solution.py
@@ -232,7 +232,10 @@
         gather(c)
         of_chunk(c, lambda p, there: fetch(p, there).start())
 
-    loop(0, chunks, gather_and_send)
+    def turned_by_core(i):
+        return lax.rem(i + core * (chunks // 2), chunks)
+
+    loop(0, chunks, lambda i: gather_and_send(turned_by_core(i)))
     got[0:CAP, :] = send[0:CAP, :]
 
     block = min(256, queries)
@@ -289,7 +292,7 @@
 
         logits(c)
 
-    loop(0, chunks, receive)
+    loop(0, chunks, lambda i: receive(turned_by_core(i)))
 
     def totals():
         pos_logit = prow[...]

time: 141 us -> 139 us (0.986)
  Pallas kernels: 140 us -> 138 us
    pallas_call x1, Pallas kernels: 137 us -> 135 us  [local(): pl.pallas_call(functools.partial(kernel, n, group), out_shape=(pltpu.VMEM...]
where the time goes in v7:
time: 139 us
  Pallas kernels  138 us (99%)
    pallas_call x1, Pallas kernels, local(): pl.pallas_call(functools.partial(kernel, n, group), out_shape=(pltpu.VMEM...  135 us
    pallas_call x1, Pallas kernels, local(): pl.pallas_call(hand_over, out_shape=(jax.ShapeDtypeStruct((1, count), f32...  3.42 us

profile of v7, /device:TPU:1, one launch (start us, length us, event | category | flops | bytes accessed | tf_op | source)
XLA Modules:
  0.0 138.6 jit_solution(15277702759980791754)
XLA Ops:
  0.6 134.5 %shard_map.67 = (f32[1,2048]{1,0:T(1,128)S(1)}, bf16[2048,1024]{1,0:T(8,128)(2,1)S(1)}, bf16[2048,1024]{1,0:T(8,128)(2,1)S(1)}) custom-call(s32[1,2048]{1,0:T(1,128)} %ids_ref.1, bf16[2048,1024]{1,0:T(8,128)(2,1)} %q_hbm.1, bf16[2048,1024]{1,0:T(8,128)(2,1)} %pos_hbm.1, bf16[2048,1024]{1,0:T(8,128)(2,1)} %pas_hbm.1), custom_call_target="tpu_custom_call" | custom-call | flops 51539607552 | bytes 41943040 | tf_op jit(solution)/shard_map/pallas_call | solution.py:430
  135.2 3.4 %shard_map.68 = (f32[1,2048]{1,0:T(1,128)}, bf16[2048,1024]{1,0:T(8,128)(2,1)}, bf16[2048,1024]{1,0:T(8,128)(2,1)}) custom-call(f32[1,2048]{1,0:T(1,128)S(1)} %get-tuple-element.9.loss, bf16[2048,1024]{1,0:T(8,128)(2,1)S(1)} %get-tuple-element.10.grad_q, bf16[2048,1024]{1,0:T(8,128)(2,1)S(1)} %get-tuple-element.11.grad_p), custom_call_target="tpu_custom_call" | custom-call | tf_op jit(solution)/shard_map/pallas_call | solution.py:471
